TPU v7x, 512 devices: a whole 4x8x8 slice. The times are simulated.
512 devices in a mesh: lon: 64 (over z_hi, y, core), lat: 8 (over x, z_lo).
Axes of the slice: x: 4, y: 8, z: 8 (z_hi: 4, z_lo: 2; z = z_hi * 2 + z_lo), core: 2. Of those that a mesh axis runs over, the one named last changes fastest.
Arguments:
- fields: bfloat16 [2, 48, 768, 192], P(None, 'lat', 'lon'), may hold values from -6 to 6
- grad_out: bfloat16 [2, 48, 768, 192], P(None, 'lat', 'lon'), may hold values from -6 to 6
- mask_ids: int32 [2, 48, 768], P(None, 'lat', 'lon'), may hold values from 0 to 2
- ln_gain: float32 [192], replicated, may hold values from 0.5 to 1.5
- qkv_weight: bfloat16 [192, 576], replicated, may hold values from -0.4375 to 0.4375
- proj_weight: bfloat16 [192, 192], replicated, may hold values from -0.4375 to 0.4375
- bias_table: float32 [8, 1, 6, 3312], P('lat'), may hold values from -6 to 6
Outputs:
- grad_fields: bfloat16 [2, 48, 768, 192], P(None, 'lat', 'lon')
- grad_qkv: float32 [192, 576], replicated
- grad_proj: float32 [192, 192], replicated
- grad_gain: float32 [192], replicated
- grad_table: float32 [8, 1, 6, 3312], P('lat')
All inputs are finite; a program needn't handle non-finite values.
Results may differ from a plain program's by a relative error of at most 0.017.
Values may be sent and summed in bfloat16 or wider, within the bound.
A program may use at most 64 MiB of HBM per device.

v0:
```python
import jax
import jax.numpy as jnp
from jax import lax
from jax.sharding import PartitionSpec as P

WIN_Z = 2
WIN_LAT = 6
WIN_LON = 12


epsilon = 1e-05


def passed_along(block, axis, distance):
    devices = range(lax.axis_size(axis))
    route = [((i - distance) % len(devices), i) for i in devices]
    return lax.ppermute(block, axis, route)


def to_windows(grid):
    level_count, row_count, col_count, channels = grid.shape
    shaped = grid.reshape(
        level_count // WIN_Z,
        WIN_Z,
        row_count // WIN_LAT,
        WIN_LAT,
        col_count // WIN_LON,
        WIN_LON,
        channels,
    )
    shaped = shaped.transpose(2, 0, 4, 1, 3, 5, 6)
    return shaped.reshape(
        row_count // WIN_LAT,
        level_count // WIN_Z,
        col_count // WIN_LON,
        WIN_Z * WIN_LAT * WIN_LON,
        channels,
    )


def from_windows(blocks, level_count, row_count, col_count):
    channels = blocks.shape[-1]
    shaped = blocks.reshape(
        row_count // WIN_LAT,
        level_count // WIN_Z,
        col_count // WIN_LON,
        WIN_Z,
        WIN_LAT,
        WIN_LON,
        channels,
    )
    shaped = shaped.transpose(1, 3, 0, 4, 2, 5, 6)
    return shaped.reshape(level_count, row_count, col_count, channels)


def lon_pairs():
    shape = (WIN_LON, WIN_LON, 2 * WIN_LON - 1)
    first = lax.broadcasted_iota(jnp.int32, shape, 0)
    second = lax.broadcasted_iota(jnp.int32, shape, 1)
    offset = lax.broadcasted_iota(jnp.int32, shape, 2)
    return (second - first + WIN_LON - 1 == offset).astype(jnp.float32)


def window_grads(field_win, grad_win, ids_win, table_win, ln_gain, qkv_weight, proj_weight):
    win_count, win_tokens, channels = field_win.shape
    head_count = table_win.shape[1]
    head_size = channels // head_count
    floats = field_win.astype(jnp.float32)
    centred = floats - jnp.mean(floats, axis=-1, keepdims=True)
    inv_std = lax.rsqrt(jnp.mean(centred * centred, axis=-1, keepdims=True) + epsilon)
    normed = centred * inv_std
    hidden = (normed * ln_gain).astype(jnp.bfloat16).reshape(win_count * win_tokens, channels)
    projected = jnp.dot(hidden, qkv_weight, preferred_element_type=jnp.float32)
    projected = projected.reshape(win_count, win_tokens, 3, head_count, head_size)
    scaling = head_size ** (-0.5)
    queries = (projected[:, :, 0] * scaling).astype(jnp.bfloat16)
    key_part = projected[:, :, 1].astype(jnp.bfloat16)
    value_part = projected[:, :, 2].astype(jnp.bfloat16)
    pairs = lon_pairs()
    table_shaped = table_win.reshape(
        win_count, head_count, WIN_Z, WIN_Z, WIN_LAT, WIN_LAT, 2 * WIN_LON - 1
    )
    bias_term = jnp.einsum("bhpqstr,ijr->bhpsiqtj", table_shaped, pairs)
    bias_term = bias_term.reshape(win_count, head_count, win_tokens, win_tokens)
    scores = (
        jnp.einsum("bihd,bjhd->bhij", queries, key_part, preferred_element_type=jnp.float32)
        + bias_term
    )
    same_id = ids_win[:, None, :, None] == ids_win[:, None, None, :]
    scores = jnp.where(same_id, scores, -1000000000.0)
    row_max = jnp.max(scores, axis=-1, keepdims=True)
    raised = jnp.exp(scores - row_max)
    attn_prob = raised / jnp.sum(raised, axis=-1, keepdims=True)
    prob_bf = attn_prob.astype(jnp.bfloat16)
    attended = jnp.einsum(
        "bhij,bjhd->bihd", prob_bf, value_part, preferred_element_type=jnp.float32
    )
    attended = attended.astype(jnp.bfloat16).reshape(win_count * win_tokens, channels)
    grad_flat = grad_win.reshape(win_count * win_tokens, channels)
    grad_proj = jnp.dot(attended.T, grad_flat, preferred_element_type=jnp.float32)
    grad_attended = jnp.dot(grad_flat, proj_weight.T, preferred_element_type=jnp.float32)
    grad_attended = grad_attended.astype(jnp.bfloat16).reshape(
        win_count, win_tokens, head_count, head_size
    )
    grad_prob = jnp.einsum(
        "bihd,bjhd->bhij", grad_attended, value_part, preferred_element_type=jnp.float32
    )
    grad_value = jnp.einsum(
        "bhij,bihd->bjhd", prob_bf, grad_attended, preferred_element_type=jnp.float32
    ).astype(jnp.bfloat16)
    grad_score = attn_prob * (grad_prob - jnp.sum(attn_prob * grad_prob, axis=-1, keepdims=True))
    score_shaped = grad_score.reshape(
        win_count, head_count, WIN_Z, WIN_LAT, WIN_LON, WIN_Z, WIN_LAT, WIN_LON
    )
    grad_table = jnp.einsum("bhpsiqtj,ijr->bhpqstr", score_shaped, pairs).reshape(
        win_count, head_count, -1
    )
    score_bf = grad_score.astype(jnp.bfloat16)
    grad_query = (
        jnp.einsum("bhij,bjhd->bihd", score_bf, key_part, preferred_element_type=jnp.float32)
        * scaling
    ).astype(jnp.bfloat16)
    grad_key = jnp.einsum(
        "bhij,bihd->bjhd", score_bf, queries, preferred_element_type=jnp.float32
    ).astype(jnp.bfloat16)
    grad_joint = jnp.stack([grad_query, grad_key, grad_value], axis=2).reshape(
        win_count * win_tokens, 3 * channels
    )
    weight_grad = jnp.dot(hidden.T, grad_joint, preferred_element_type=jnp.float32)
    grad_hidden = jnp.dot(grad_joint, qkv_weight.T, preferred_element_type=jnp.float32).reshape(
        win_count, win_tokens, channels
    )
    grad_gain = jnp.sum(grad_hidden * normed, axis=(0, 1))
    scaled_grad = grad_hidden * ln_gain
    grad_local = inv_std * (
        scaled_grad
        - jnp.mean(scaled_grad, axis=-1, keepdims=True)
        - normed * jnp.mean(scaled_grad * normed, axis=-1, keepdims=True)
    )
    return (grad_local.astype(jnp.bfloat16), weight_grad, grad_proj, grad_gain, grad_table)


def body(fields, grad_out, mask_ids, ln_gain, qkv_weight, proj_weight, bias_table):
    cut_lon = WIN_LON // 2
    cut_lat = WIN_LAT // 2
    cut_level = WIN_Z // 2
    level_count, row_count, col_count, channels = fields.shape
    arrived = passed_along((fields[:, :, :cut_lon], grad_out[:, :, :cut_lon]), "lon", -1)
    moved = jnp.concatenate([fields[:, :, cut_lon:], arrived[0]], axis=2)
    moved_grad = jnp.concatenate([grad_out[:, :, cut_lon:], arrived[1]], axis=2)
    below = passed_along((moved[:, :cut_lat], moved_grad[:, :cut_lat]), "lat", -1)
    moved = jnp.concatenate([moved[:, cut_lat:], below[0]], axis=1)
    moved_grad = jnp.concatenate([moved_grad[:, cut_lat:], below[1]], axis=1)
    moved = jnp.roll(moved, -cut_level, 0)
    moved_grad = jnp.roll(moved_grad, -cut_level, 0)
    field_win = to_windows(moved)
    lat_win, z_win, lon_win, win_tokens = field_win.shape[:4]
    total_win = lat_win * z_win * lon_win
    table_tail = bias_table.shape[2:]
    grad_win = to_windows(moved_grad).reshape(total_win, win_tokens, channels)
    ids_win = to_windows(mask_ids[..., None])[..., 0].reshape(total_win, win_tokens)
    table_win = bias_table[:, :, None].reshape((total_win,) + table_tail)
    grad_local, weight_grad, grad_proj, grad_gain, grad_table = window_grads(
        field_win.reshape(total_win, win_tokens, channels),
        grad_win,
        ids_win,
        table_win,
        ln_gain,
        qkv_weight,
        proj_weight,
    )
    grad_table = jnp.sum(grad_table.reshape((lat_win, z_win, lon_win) + table_tail), axis=2)
    local_grid = from_windows(
        grad_local.reshape(lat_win, z_win, lon_win, win_tokens, channels),
        level_count,
        row_count,
        col_count,
    )
    local_grid = jnp.roll(local_grid, cut_level, 0)
    received = passed_along(local_grid[:, row_count - cut_lat :], "lat", 1)
    local_grid = jnp.concatenate([received, local_grid[:, : row_count - cut_lat]], axis=1)
    received = passed_along(local_grid[:, :, col_count - cut_lon :], "lon", 1)
    local_grid = jnp.concatenate([received, local_grid[:, :, : col_count - cut_lon]], axis=2)
    grad_fields = (grad_out.astype(jnp.float32) + local_grid.astype(jnp.float32)).astype(
        jnp.bfloat16
    )
    grad_table = lax.psum(grad_table, "lon")
    weight_grad, grad_proj, grad_gain = lax.psum(
        (weight_grad, grad_proj, grad_gain), ("lon", "lat")
    )
    return (grad_fields, weight_grad, grad_proj, grad_gain, grad_table)


def solution(mesh):
    placed = (
        P(None, "lat", "lon", None),
        P(None, "lat", "lon", None),
        P(None, "lat", "lon"),
        P(),
        P(),
        P(),
        P("lat", None, None, None),
    )
    return jax.shard_map(
        body,
        mesh=mesh,
        in_specs=placed,
        out_specs=(P(None, "lat", "lon", None), P(), P(), P(), P("lat", None, None, None)),
        check_vma=False,
    )
```

profile of v0, /device:TPU:1, one launch (start us, length us, event | category | flops | bytes accessed | tf_op | source)
XLA Modules:
  0.0 851.2 jit_solution(6060069225609935517)
XLA Ops:
  8.1 8.8 %collective-permute-start = (bf16[2,6,6,192]{3,0,2,1:T(2,128)(2,1)S(1)}, bf16[2,6,6,192]{3,0,2,1:T(2,128)(2,1)S(1)}, u32[]{:S(2)}, u32[]{:S(2)}) collective-permute-start(bf16[2,6,6,192]{3,0,2,1:T(2,128)(2,1)S(1)} %get-tuple-element.33), channel_id=1, source_target_pairs={{8,0},{16,8},{24,16},{32,24},{40,32},{48,40},{56,48},{64,56},{72,6... | collective-permute-start | bytes 82952 | tf_op jit(solution)/shard_map/ppermute | solution.py:17
  17.7 7.9 collective-permute-start.2
  25.6 1.1 reduce.14
  28.0 4.0 convolution_bitcast_fusion
  32.0 11.3 %copy.74 = f32[1,6,2,6,12,2,6,12]{4,3,2,7,6,5,1,0:T(8,128)} copy(f32[1,6,2,6,12,2,6,12]{7,6,3,5,2,1,4,0:T(8,128)} %convolution_bitcast_fusion) | data formatting | bytes 995328 | tf_op jit(solution)/shard_map/reshape | solution.py:84
  43.3 5.0 reshape.420
  48.6 5.3 collective-permute-start.1
  54.1 2.2 collective-permute-start.3
  57.2 1.6 collective-permute-done.3
  62.7 1.9 fusion.7
  64.6 1.2 multiply_reduce_fusion
  66.2 1.1 fusion.5
  67.3 1.3 convolution_convert_fusion
  68.6 4.4 reshape.421
  73.8 1.9 collective-permute-start.4
  76.8 9.7 %copy.63 = bf16[6,2,6,12,2,6,12]{6,5,3,4,2,1,0:T(8,128)(2,1)} copy(bf16[6,2,6,12,2,6,12]{3,2,1,6,5,4,0:T(8,128)(2,1)} %reshape.421) | data formatting | bytes 497664 | tf_op jit(solution)/shard_map/reshape.48
  86.5 3.1 convolution_bitcast_fusion.1
  91.9 1.9 collective-permute-start.5
  93.9 103.3 %psum.30 = f32[192]{0:T(256)} all-reduce(f32[192]{0:T(256)S(1)} %get-tuple-element.15), channel_id=1, replica_groups=mesh['lon'=64,'lat'=8] {'lon','lat'}, use_global_device_ids=true, to_apply=%region_10.11 | all-reduce | flops 192 | bytes 1536 | tf_op jit(solution)/shard_map/psum | solution.py:188
  197.9 367.5 %all-reduce.4.cloned.1.call-done = f32[1,1,6,3312]{3,0,2,1:T(1,128)} async-done(((f32[1,1,6,3312]{3,0,2,1:T(1,128)}), f32[1,1,6,3312]{3,0,2,1:T(1,128)}) %all-reduce.4.cloned.1.call-update) | async-done | bytes 79504 | tf_op jit(solution)/shard_map/psum | solution.py:187
  565.4 274.0 %all-reduce.6.cloned.1.call-done = (f32[192,576]{1,0:T(8,128)}, f32[192,192]{1,0:T(8,128)}) async-done(((f32[192,576]{1,0:T(8,128)}, f32[192,192]{1,0:T(8,128)}), (f32[192,576]{1,0:T(8,128)}, f32[192,192]{1,0:T(8,128)})) %all-reduce.6.cloned.1.call-update) | async-done | bytes 589840 | tf_op jit(solution)/shard_map/psum | solution.py:188
  839.4 1.8 copy.81
  841.3 1.6 copy.82
  842.9 1.5 copy.83
  (74 shorter events, 13.4 us)
Async XLA Ops:
  7.2 52.0 %copy-start = (bf16[192,192]{1,0:T(8,128)(2,1)S(1)}, bf16[192,192]{1,0:T(8,128)(2,1)}, u32[]{:S(2)}) copy-start(bf16[192,192]{1,0:T(8,128)(2,1)} %param.12) | copy-start | bytes 221188
  7.2 558.2 %all-reduce.4.cloned.1.call-start = ((), (), s32[]{:S(2)}) async-start(), calls=%async_computation | async-start | bytes 159744 | tf_op jit(solution)/shard_map/psum | solution.py:187
  8.1 40.4 %collective-permute-start = (bf16[2,6,6,192]{3,0,2,1:T(2,128)(2,1)S(1)}, bf16[2,6,6,192]{3,0,2,1:T(2,128)(2,1)S(1)}, u32[]{:S(2)}, u32[]{:S(2)}) collective-permute-start(bf16[2,6,6,192]{3,0,2,1:T(2,128)(2,1)S(1)} %get-tuple-element.33), channel_id=1, source_target_pairs={{8,0},{16,8},{24,16},{32,24},{40,32},{48,40},{56,48},{64,56},{72,6... | collective-permute-start | bytes 82952 | tf_op jit(solution)/shard_map/ppermute | solution.py:17
  17.7 36.2 %collective-permute-start.2 = (bf16[2,6,6,192]{3,0,2,1:T(2,128)(2,1)S(1)}, bf16[2,6,6,192]{3,0,2,1:T(2,128)(2,1)S(1)}, u32[]{:S(2)}, u32[]{:S(2)}) collective-permute-start(bf16[2,6,6,192]{3,0,2,1:T(2,128)(2,1)S(1)} %get-tuple-element.29), channel_id=1, source_target_pairs={{8,0},{16,8},{24,16},{32,24},{40,32},{48,40},{56,48},{64,56},{72,6... | collective-permute-start | bytes 82952 | tf_op jit(solution)/shard_map/ppermute | solution.py:17
  43.3 5.0 copy-start.1
  48.3 12.0 %copy-start.6 = (f32[192]{0:T(256)S(1)}, f32[192]{0:T(256)}, u32[]{:S(2)}) copy-start(f32[192]{0:T(256)} %param.10) | copy-start | bytes 2308
  48.6 7.6 collective-permute-start.1
  54.1 4.7 collective-permute-start.3
  60.9 0.7 copy-start.2
  61.9 2.7 copy-start.5
  67.3 5.7 copy-start.4
  73.8 17.9 %collective-permute-start.4 = (bf16[2,3,12,192]{3,0,2,1:T(2,128)(2,1)S(1)}, bf16[2,3,12,192]{3,0,2,1:T(2,128)(2,1)S(1)}, u32[]{:S(2)}, u32[]{:S(2)}) collective-permute-start(bf16[2,3,12,192]{3,0,2,1:T(2,128)(2,1)S(1)} %fusion.25), channel_id=1, source_target_pairs={{7,0},{0,1},{1,2},{2,3},{3,4},{4,5},{5,6},{6,7},{15,8},{8,9},{9,10... | collective-permute-start | bytes 82952 | tf_op jit(solution)/shard_map/ppermute | solution.py:17
  86.5 110.6 %copy-start.3 = (bf16[2,6,12,192]{3,0,2,1:T(2,128)(2,1)S(1)}, bf16[2,6,12,192]{3,0,2,1:T(2,128)(2,1)}, u32[]{:S(2)}) copy-start(bf16[2,6,12,192]{3,0,2,1:T(2,128)(2,1)} %param.8) | copy-start | bytes 165892
  90.8 748.6 %all-reduce.6.cloned.1.call-start = ((), (), s32[]{:S(2)}) async-start(), calls=%async_computation.1 | async-start | bytes 1376256 | tf_op jit(solution)/shard_map/psum | solution.py:188
  91.9 105.3 %collective-permute-start.5 = (bf16[2,6,6,192]{3,0,2,1:T(2,128)(2,1)S(1)}, bf16[2,6,6,192]{3,0,2,1:T(2,128)(2,1)S(1)}, u32[]{:S(2)}, u32[]{:S(2)}) collective-permute-start(bf16[2,6,6,192]{3,0,2,1:T(2,128)(2,1)S(1)} %get-tuple-element.22), channel_id=1, source_target_pairs={{504,0},{0,8},{8,16},{16,24},{24,32},{32,40},{40,48},{48,56},{56,6... | collective-permute-start | bytes 82952 | tf_op jit(solution)/shard_map/ppermute | solution.py:17
Sparse Core Ops, SparseCore 0:
  90.9 474.4 all-reduce.3
  572.0 267.4 all-reduce.5
where the time goes:
time: 852 us; the launch traced here: 851 us
  waiting for transfers between devices  643 us (75%)
  blocking collectives  103 us (12%)
  local copies, waits for them, and re-layouts  41.7 us (5%)
  starting transfers between devices  28.1 us (3%)
  matrix products  15.9 us (2%)
  between operations  14.4 us (2%)
    psum x1, waiting for transfers between devices, body(): grad_table = lax.psum(grad_table, 'lon')  367 us
    psum x1, waiting for transfers between devices, body(): lax.psum((weight_grad, grad_proj, grad_gain), ('lon', 'lat'))  274 us
    psum x1, blocking collectives, body(): lax.psum((weight_grad, grad_proj, grad_gain), ('lon', 'lat'))  103 us
    ppermute x6, starting transfers between devices, passed_along(): return lax.ppermute(block, axis, route)  28 us
  transfers between devices with their start and end apart: 8, of which 3 were waited for; matrix products, arithmetic and copies ran while one was open for 5% of the time, Pallas kernels for 0%

commit v1 on v0

v1 whole, which is shorter than its diff:
```python
import functools

import jax
import jax.numpy as jnp
import numpy as np
from jax import lax
from jax.experimental import pallas as pl
from jax.experimental.pallas import tpu as pltpu
from jax.sharding import PartitionSpec as P

D = 192
HEADS = 6
LON = 12
CELLS = 12
TOK = 144
SPAN = 23 * CELLS
SEG = 138
EPS = 1e-05
MESH = pl.DeviceIdType.MESH
BF = jnp.bfloat16
F32 = jnp.float32

NX, NY, NZH, NZL, NC = 4, 8, 4, 2, 2
GROUP = 8


def token_tables():
    gather = np.zeros((TOK, 384), np.float32)
    scatter = np.zeros((192, TOK), np.float32)
    for o in range(12):
        for z in range(2):
            for a in range(6):
                t = o * 12 + z * 6 + a
                s = (a >= 3) * 2 + (o >= 6)
                zs = (z + 1) % 2
                gather[t, s * 96 + (zs * 3 + a % 3) * 16 + (o + 6) % 12] = 1
                scatter[s * 48 + (zs * 3 + a % 3) * 6 + o % 6, t] = 1
    place = np.zeros((192, 192), np.float32)
    for z in range(2):
        for a in range(6):
            for o in range(12):
                s = (a < 3) * 2 + (o < 6)
                place[(z * 6 + a) * 16 + o, s * 48 + (z * 3 + a % 3) * 6 + o % 6] = 1
    shear = np.zeros((512, 384), np.float32)
    for zq in range(2):
        for aq in range(6):
            for r in range(23):
                shear[zq * 256 + aq * 23 + r, r * 12 + zq * 6 + aq] = 1
    row_of = np.zeros((TOK, 16), np.float32)
    lon_of = np.zeros((TOK, 128), np.float32)
    for t in range(TOK):
        row_of[t, t % 12] = 1
        lon_of[t, t // 12] = 1
    return gather, scatter, place, shear, row_of, lon_of


def dot(a, b):
    return lax.dot_general(a, b, (((1,), (0,)), ((), ())), preferred_element_type=F32)


def dot_rows(a, b):
    return lax.dot_general(a, b, (((1,), (1,)), ((), ())), preferred_element_type=F32)


def dot_cols(a, b):
    return lax.dot_general(a, b, (((0,), (0,)), ((), ())), preferred_element_type=F32)


def split(v):
    hi = v.astype(BF)
    return hi, (v - hi.astype(F32)).astype(BF)


def expand_bias(table, shear, xs, bias):
    for zp in range(2):
        for zq in range(2):
            for ap in range(6):
                start = ((zp * 2 + zq) * 6 + ap) * SEG
                rows = pl.ds(zp * 6 + ap, HEADS, stride=CELLS)
                part = table[0, 0, :, start : start + SEG]
                rest = jnp.concatenate([part[:, 128:], jnp.zeros((HEADS, 256 - SEG), F32)], axis=1)
                xs[2 * zq, rows, :] = part[:, 0:128]
                xs[2 * zq + 1, rows, :] = rest
    hi, lo = split(jnp.concatenate([xs[k] for k in range(4)], axis=1))
    sheared = dot(hi, shear[...]) + dot(lo, shear[...])
    for op in range(LON):
        window = sheared[:, (11 - op) * 12 : (11 - op) * 12 + TOK]
        for h in range(HEADS):
            bias[h, op * 12 : (op + 1) * 12, :] = window[h * 12 : (h + 1) * 12]


def fold_bias(gs, shear, stacked, xs, flat):
    for op in range(LON):
        for h in range(HEADS):
            stacked[op, h * 12 : (h + 1) * 12, :] = gs[h, op * 12 : (op + 1) * 12, :]
    total = None
    for op in range(LON):
        left = (11 - op) * 12
        parts = [stacked[op]]
        if left:
            parts.insert(0, jnp.zeros((72, left), F32))
        if SPAN - left - TOK:
            parts.append(jnp.zeros((72, SPAN - left - TOK), F32))
        piece = jnp.concatenate(parts, axis=1) if len(parts) > 1 else parts[0]
        total = piece if total is None else total + piece
    total = jnp.concatenate([total, jnp.zeros((72, 384 - SPAN), F32)], axis=1)
    hi, lo = split(total)
    spread = dot_rows(hi, shear[...]) + dot_rows(lo, shear[...])
    for k in range(4):
        xs[k] = spread[:, 128 * k : 128 * k + 128]
    for zp in range(2):
        for zq in range(2):
            for ap in range(6):
                start = ((zp * 2 + zq) * 6 + ap) * SEG
                rows = pl.ds(zp * 6 + ap, HEADS, stride=CELLS)
                flat[0:HEADS, start : start + 128] = xs[2 * zq, rows, :]
                flat[0:HEADS, start + 128 : start + SEG] = xs[2 * zq + 1, rows, :][:, 0 : SEG - 128]


def window_ids(ids, row_of, lon_of, ms):
    ms[...] = jnp.zeros_like(ms)
    ms[0:6, 0:12] = ids[0].astype(F32)
    ms[6:12, 0:12] = ids[1].astype(F32)
    m = ms[...].astype(BF)
    column = jnp.sum(dot(row_of[...], m) * lon_of[...].astype(F32), axis=1, keepdims=True)
    spread = dot_cols(m, row_of[...].astype(F32).T.astype(BF))
    row = jnp.sum(spread * lon_of[...].astype(F32).T, axis=0, keepdims=True)
    return column, row


def copy_slabs(received, s, slabs):
    for z in range(2):
        for a in range(3):
            row = (s * 6 + z * 3 + a) * 16
            slabs[row : row + 12, :] = received[s, z, a]


def window_grads(x, g, same, gain, wqkv, wproj, bias, gs_out):
    x = x.astype(F32)
    centred = x - jnp.mean(x, axis=-1, keepdims=True)
    inv_std = lax.rsqrt(jnp.mean(centred * centred, axis=-1, keepdims=True) + EPS)
    normed = centred * inv_std
    hidden = (normed * gain).astype(BF)
    projected = dot(hidden, wqkv)
    scaling = 32 ** (-0.5)
    query = (projected[:, :D] * scaling).astype(BF)
    key = projected[:, D : 2 * D].astype(BF)
    value = projected[:, 2 * D :].astype(BF)
    grad_att = dot_rows(g, wproj).astype(BF)
    lane = lax.broadcasted_iota(jnp.int32, (TOK, D), 1) // 32
    zero = jnp.zeros((TOK, D), BF)
    attended = dv = dq = dk = None

    def add(total, term):
        return term if total is None else total + term

    for h in range(HEADS):
        mine = lane == h
        qh = jnp.where(mine, query, zero)
        kh = jnp.where(mine, key, zero)
        vh = jnp.where(mine, value, zero)
        gh = jnp.where(mine, grad_att, zero)
        scores = jnp.where(same, dot_rows(qh, key) + bias[h], -1000000000.0)
        raised = jnp.exp(scores - jnp.max(scores, axis=-1, keepdims=True))
        prob = raised * (1.0 / jnp.sum(raised, axis=-1, keepdims=True))
        prob_bf = prob.astype(BF)
        attended = add(attended, dot(prob_bf, vh))
        grad_prob = dot_rows(gh, value)
        dv = add(dv, dot_cols(prob_bf, gh))
        weighted = prob * grad_prob
        gs = weighted - prob * jnp.sum(weighted, axis=-1, keepdims=True)
        gs_out[h] = gs
        gs = gs.astype(BF)
        dq = add(dq, dot(gs, kh))
        dk = add(dk, dot_cols(gs, qh))
    joint = jnp.concatenate(
        [(dq * scaling).astype(BF), dk.astype(BF), dv.astype(BF)], axis=1
    )
    grad_qkv = dot_cols(hidden, joint)
    grad_proj = dot_cols(attended.astype(BF), g)

    def local():
        grad_hidden = dot_rows(joint, wqkv)
        scaled = grad_hidden * gain
        return (
            inv_std
            * (
                scaled
                - jnp.mean(scaled, axis=-1, keepdims=True)
                - normed * jnp.mean(scaled * normed, axis=-1, keepdims=True)
            )
        ).astype(BF)

    return grad_qkv, grad_proj, local


def pack_weights(grad_qkv, grad_proj, flat):
    for c in range(4):
        flat[c * 192 : (c + 1) * 192, :] = grad_qkv[:, c * 128 : (c + 1) * 128].astype(BF)
    last = jnp.concatenate([grad_qkv[:, 512:576], grad_proj[:, 128:192]], axis=1)
    flat[768:960, :] = last.astype(BF)
    flat[960:1152, :] = grad_proj[:, 0:128].astype(BF)


def finish_weights(flat, wqkv, gain, out_qkv, out_proj, out_gain):
    for c in range(4):
        out_qkv[:, c * 128 : (c + 1) * 128] = flat[c * 192 : (c + 1) * 192, :].astype(F32)
    last = flat[768:960, :].astype(F32)
    out_qkv[:, 512:576] = last[:, 0:64]
    out_proj[:, 128:192] = last[:, 64:128]
    out_proj[:, 0:128] = flat[960:1152, :].astype(F32)
    products = out_qkv[...] * wqkv[...].astype(F32)
    hi, lo = split(products)
    ones = jnp.ones((8, 576), BF)
    row = (dot_rows(ones, hi) + dot_rows(ones, lo))[0:1]
    out_gain[...] = (row / gain[...].reshape(1, D)).reshape(D)


def finish_fields(quadrants, place, grad_out, out):
    blocks = dot(place[...], quadrants)
    for z in range(2):
        for a in range(6):
            row = (z * 6 + a) * 16
            own = grad_out[z, a].astype(F32)
            out[z, a] = (own + blocks[row : row + 12]).astype(BF)


def finish_table(rows, out):
    for k in range(26):
        width = min(128, 3312 - 128 * k)
        out[0, 0, :, 128 * k : 128 * k + width] = rows[8 * k : 8 * k + HEADS, 0:width].astype(F32)


def exchange(src_of, recv, rank, device_of, sends, recvs):
    copies = []
    for k in range(1, GROUP):
        peer = lax.rem(rank + k, GROUP)
        copy = pltpu.make_async_remote_copy(
            src_ref=src_of(peer),
            dst_ref=recv.at[rank],
            send_sem=sends.at[k],
            recv_sem=recvs.at[k],
            device_id=device_of(peer),
            device_id_type=MESH,
        )
        copy.start()
        copies.append(copy)
    return copies


def arrive(copies):
    for copy in copies:
        copy.wait_recv()


def total_of(recv):
    total = recv[0].astype(F32)
    for k in range(1, GROUP):
        total = total + recv[k].astype(F32)
    return total


def kernel(
    fields, grad_out, ids, gain, wqkv, wproj, table,
    gather, scatter, place, shear, row_of, lon_of,
    out_flat, out_quads, out_table,
    field_in, grad_in, slabs_f, slabs_g, xs, bias, gs, stacked, ms, tflat, quads_out, quads_in,
    w_out, w1, w2_out, w2, w3_out, w3, w4, w5,
    t1_out, t1, t2_out, t2, t3,
    own_sem, halo_send, halo_recv, back_send, back_recv, sends, recvs,
):
    l, a = lax.axis_index("lon"), lax.axis_index("lat")
    core, y, zh = lax.rem(l, NC), lax.rem(l // NC, NY), l // (NC * NY)
    x, zl = a // NZL, lax.rem(a, NZL)
    near_l, far_l = lax.rem(l + 63, 64), lax.rem(l + 1, 64)
    near_a, far_a = lax.rem(a + 7, 8), lax.rem(a + 1, 8)

    def lon(zh, y, core):
        return (zh * NY + y) * NC + core

    def by_xc(r):
        return (lon(zh, y, lax.rem(r, NC)), (r // NC) * NZL + zl)

    def by_y(r):
        return (lon(zh, r, core), a)

    def by_z(r):
        return (lon(r // NZL, y, core), x * NZL + lax.rem(r, NZL))

    def by_zc(r):
        return (lon(r // NC, y, lax.rem(r, NC)), a)

    groups = (
        (x * NC + core, by_xc),
        (y, by_y),
        (zh * NZL + zl, by_z),
        (zh * NC + core, by_zc),
    )
    barrier = pltpu.get_barrier_semaphore()
    near = ((near_l, a), (l, near_a), (near_l, near_a))
    far = ((far_l, a), (l, far_a), (far_l, far_a))
    for device in near + far:
        pl.semaphore_signal(barrier, inc=1, device_id=device, device_id_type=MESH)
    for rank, device_of in groups:
        for k in range(1, GROUP):
            pl.semaphore_signal(
                barrier, inc=1, device_id=device_of(lax.rem(rank + k, GROUP)), device_id_type=MESH
            )
    owns = []
    for k, (src, dst) in enumerate(((fields, field_in), (grad_out, grad_in))):
        own = pltpu.make_async_copy(src.at[:, 3:6], dst.at[0], own_sem.at[k])
        own.start()
        owns.append(own)
    pl.semaphore_wait(barrier, 6 + 7 * len(groups))

    halo = []
    for s in range(1, 4):
        rows = slice(3, 6) if s == 1 else slice(0, 3)
        for k, (src, dst) in enumerate(((fields, field_in), (grad_out, grad_in))):
            copy = pltpu.make_async_remote_copy(
                src_ref=src.at[:, rows],
                dst_ref=dst.at[s],
                send_sem=halo_send.at[2 * s + k],
                recv_sem=halo_recv.at[2 * s + k],
                device_id=near[s - 1],
                device_id_type=MESH,
            )
            copy.start()
            halo.append(copy)

    slabs_f[...] = jnp.zeros_like(slabs_f)
    slabs_g[...] = jnp.zeros_like(slabs_g)
    expand_bias(table, shear, xs, bias)
    column, row = window_ids(ids, row_of, lon_of, ms)
    same = column == row

    for own in owns:
        own.wait()
    copy_slabs(field_in, 0, slabs_f)
    copy_slabs(grad_in, 0, slabs_g)
    arrive(halo)
    for s in range(1, 4):
        copy_slabs(field_in, s, slabs_f)
        copy_slabs(grad_in, s, slabs_g)
    moved = dot(gather[...], slabs_f[...]).astype(BF)
    moved_grad = dot(gather[...], slabs_g[...]).astype(BF)
    grad_qkv, grad_proj, local = window_grads(
        moved, moved_grad, same, gain[...].reshape(1, D), wqkv[...], wproj[...], bias, gs
    )

    pack_weights(grad_qkv, grad_proj, w_out)
    started = []

    def go(index, src_of, recv, group, local_src):
        rank, device_of = groups[group]
        copies = exchange(src_of, recv, rank, device_of, sends.at[index], recvs.at[index])
        started.extend(copies)
        recv[rank] = local_src(rank)
        return copies

    def block(ref, size):
        return lambda r: ref.at[pl.ds(pl.multiple_of(r * size, size), size)]

    def block_value(ref, size):
        return lambda r: ref[pl.ds(pl.multiple_of(r * size, size), size), :]

    c1 = go(0, block(w_out, 144), w1, 0, block_value(w_out, 144))

    quads = dot(scatter[...], local()).astype(BF)
    quads_out[...] = quads.reshape(4, 48, D)
    back = []
    for s in range(1, 4):
        copy = pltpu.make_async_remote_copy(
            src_ref=quads_out.at[s],
            dst_ref=quads_in.at[s],
            send_sem=back_send.at[s],
            recv_sem=back_recv.at[s],
            device_id=far[s - 1],
            device_id_type=MESH,
        )
        copy.start()
        back.append(copy)
    quads_in[0] = quads_out[0]

    tflat[...] = jnp.zeros_like(tflat)
    fold_bias(gs, shear, stacked, xs, tflat)
    rows = jnp.concatenate([tflat[:, 128 * k : 128 * (k + 1)] for k in range(26)], axis=0)
    t1_out[0:208, :] = rows.astype(BF)
    t1_out[208:256, :] = jnp.zeros((48, 128), BF)
    d1 = go(1, block(t1_out, 32), t1, 1, block_value(t1_out, 32))

    arrive(c1)
    sum1 = total_of(w1).astype(BF)
    for k in range(8):
        w2_out[k, 0:16] = sum1[16 * k : 16 * k + 16]
        w2_out[k, 16:32] = sum1[128:144] if k == 0 else jnp.zeros((16, 128), BF)
    c2 = go(2, lambda r: w2_out.at[r], w2, 1, lambda r: w2_out[r])

    arrive(d1)
    t2_out[...] = total_of(t1).astype(BF)
    d2 = go(3, lambda r: t2_out, t2, 3, lambda r: t2_out[...])

    arrive(c2)
    w3_out[...] = total_of(w2).astype(BF)
    c3 = go(4, lambda r: w3_out, w3, 2, lambda r: w3_out[...])

    arrive(d2)
    t2_out2 = total_of(t2).astype(BF)
    rank_y = groups[1][0]
    t3[rank_y] = t2_out2
    d3 = exchange(lambda r: t3.at[rank_y], t3, rank_y, by_y, sends.at[5], recvs.at[5])
    started.extend(d3)

    arrive(c3)
    w4[rank_y] = total_of(w3).astype(BF)
    c4 = exchange(lambda r: w4.at[rank_y], w4, rank_y, by_y, sends.at[6], recvs.at[6])
    started.extend(c4)
    arrive(c4)
    rank_xc = groups[0][0]
    for k in range(8):
        w5[rank_xc, 16 * k : 16 * k + 16] = w4[k, 0:16]
    w5[rank_xc, 128:144] = w4[0, 16:32]
    c5 = exchange(lambda r: w5.at[rank_xc], w5, rank_xc, by_xc, sends.at[7], recvs.at[7])
    started.extend(c5)

    arrive(d3)
    for k in range(8):
        out_table[32 * k : 32 * k + 32, :] = t3[k]
    arrive(back)
    out_quads[...] = quads_in[...].reshape(192, D)
    arrive(c5)
    for k in range(8):
        out_flat[144 * k : 144 * k + 144, :] = w5[k]
    for copy in halo + back + started:
        copy.wait_send()


def finish(flat, quads, trows, grad_out, place, wqkv, gain, out_f, out_qkv, out_proj, out_gain, out_t):
    finish_weights(flat, wqkv, gain, out_qkv, out_proj, out_gain)
    finish_fields(quads[...], place, grad_out, out_f)
    finish_table(trows, out_t)


def body(fields, grad_out, mask_ids, ln_gain, qkv_weight, proj_weight, bias_table):
    consts = [jnp.asarray(v, BF) for v in token_tables()]
    vmem = pl.BlockSpec(memory_space=pltpu.VMEM)
    hbm = pl.BlockSpec(memory_space=pl.ANY)
    dma = pltpu.SemaphoreType.DMA
    scratch = [
        pltpu.VMEM((4, 2, 3, 12, D), BF),
        pltpu.VMEM((4, 2, 3, 12, D), BF),
        pltpu.VMEM((384, D), BF),
        pltpu.VMEM((384, D), BF),
        pltpu.VMEM((4, 72, 128), F32),
        pltpu.VMEM((HEADS, TOK, TOK), F32),
        pltpu.VMEM((HEADS, TOK, TOK), F32),
        pltpu.VMEM((LON, 72, TOK), F32),
        pltpu.VMEM((16, 128), F32),
        pltpu.VMEM((8, 3328), F32),
        pltpu.VMEM((4, 48, D), BF),
        pltpu.VMEM((4, 48, D), BF),
        pltpu.VMEM((1152, 128), BF),
        pltpu.VMEM((8, 144, 128), BF),
        pltpu.VMEM((8, 32, 128), BF),
        pltpu.VMEM((8, 32, 128), BF),
        pltpu.VMEM((32, 128), BF),
        pltpu.VMEM((8, 32, 128), BF),
        pltpu.VMEM((8, 32, 128), BF),
        pltpu.VMEM((8, 144, 128), BF),
        pltpu.VMEM((256, 128), BF),
        pltpu.VMEM((8, 32, 128), BF),
        pltpu.VMEM((32, 128), BF),
        pltpu.VMEM((8, 32, 128), BF),
        pltpu.VMEM((8, 32, 128), BF),
        dma((2,)),
        dma((8,)),
        dma((8,)),
        dma((4,)),
        dma((4,)),
        dma((8, 8)),
        dma((8, 8)),
    ]
    flat, quads, trows = pl.pallas_call(
        kernel,
        out_shape=(
            jax.ShapeDtypeStruct((1152, 128), BF),
            jax.ShapeDtypeStruct((192, D), BF),
            jax.ShapeDtypeStruct((256, 128), BF),
        ),
        in_specs=[hbm, hbm] + [vmem] * 11,
        out_specs=(vmem, vmem, vmem),
        scratch_shapes=scratch,
        compiler_params=pltpu.CompilerParams(
            collective_id=0, has_side_effects=True, vmem_limit_bytes=32 * 1024 * 1024
        ),
    )(fields, grad_out, mask_ids, ln_gain, qkv_weight, proj_weight, bias_table, *consts)
    place = consts[2]
    out_f, out_qkv, out_proj, out_gain, out_t = pl.pallas_call(
        finish,
        out_shape=(
            jax.ShapeDtypeStruct((2, 6, 12, D), BF),
            jax.ShapeDtypeStruct((D, 576), F32),
            jax.ShapeDtypeStruct((D, D), F32),
            jax.ShapeDtypeStruct((D,), F32),
            jax.ShapeDtypeStruct((1, 1, HEADS, 3312), F32),
        ),
        in_specs=[vmem] * 7,
        out_specs=(vmem,) * 5,
        compiler_params=pltpu.CompilerParams(vmem_limit_bytes=32 * 1024 * 1024),
    )(flat, quads, trows, grad_out, place, qkv_weight, ln_gain)
    return out_f, out_qkv, out_proj, out_gain, out_t


def solution(mesh):
    placed = (
        P(None, "lat", "lon", None),
        P(None, "lat", "lon", None),
        P(None, "lat", "lon"),
        P(),
        P(),
        P(),
        P("lat", None, None, None),
    )
    return jax.shard_map(
        body,
        mesh=mesh,
        in_specs=placed,
        out_specs=(P(None, "lat", "lon", None), P(), P(), P(), P("lat", None, None, None)),
        check_vma=False,
    )
```

time: 852 us -> 61.7 us (0.07)
  waiting for transfers between devices: 643 us -> 0 us
  blocking collectives: 103 us -> 0 us
  Pallas kernels: 0 us -> 52.8 us
  local copies, waits for them, and re-layouts: 41.7 us -> 7.76 us
  starting transfers between devices: 28.1 us -> 0 us
  matrix products: 15.9 us -> 0 us
  between operations: 14.4 us -> 0.75 us
    psum x2 -> x0, waiting for transfers between devices: 641 us -> none  [the longest x1 367 us: body(): grad_table = lax.psum(grad_table, 'lon')]
    psum x1 -> x0, blocking collectives: 103 us -> none  [body(): lax.psum((weight_grad, grad_proj, grad_gain), ('lon', 'lat'))]
    pallas_call x0 -> x2, Pallas kernels: none -> 52.8 us  [the longest x1 51.7 us: body(): pl.pallas_call(kernel, out_shape=(jax.ShapeDtypeStruct((1152, 128), BF),...]
    ppermute x6 -> x0, starting transfers between devices: 28 us -> none  [passed_along(): return lax.ppermute(block, axis, route)]
    reshape x2 -> x0, local copies, waits for them, and re-layouts: 16.3 us -> none  [window_grads(): bias_term = bias_term.reshape(win_count, head_count, win_tokens, win_tokens)]
    dot_general x13 -> x0, matrix products: 15.9 us -> none  [the longest x1 4.01 us: window_grads(): bias_term = jnp.einsum('bhpqstr,ijr->bhpsiqtj', table_shaped, pairs)]
    another operation x4 -> x0, local copies, waits for them, and re-layouts: 14.5 us -> none
  transfers between devices with their start and end apart: 8 -> 0, of which waited for: 3 -> 0; matrix products, arithmetic and copies ran while one was open for 5% -> 0% of each run, Pallas kernels for 0% -> 0%
where the time goes in v1:
time: 61.7 us; the launch traced here: 61.4 us
  Pallas kernels  52.8 us (86%)
  local copies, waits for them, and re-layouts  7.76 us (13%)
  between operations  0.75 us (1%)
    pallas_call x1, Pallas kernels, body(): pl.pallas_call(kernel, out_shape=(jax.ShapeDtypeStruct((1152, 128), BF),...  51.7 us
    unnamed x22, local copies, waits for them, and re-layouts  6.33 us
    pallas_call x2, local copies, waits for them, and re-layouts, body(): pl.pallas_call(finish, out_shape=(jax.ShapeDtypeStruct((2, 6, 12, D), BF)...  1.43 us

profile of v1, /device:TPU:1, one launch (start us, length us, event | category | flops | bytes accessed | tf_op | source)
XLA Modules:
  0.0 61.4 jit_solution(9186730317518922054)
XLA Ops:
  0.6 0.7 %copy.20.ids = s32[2,6,12]{2,1,0:T(8,128)S(1)} copy(s32[2,6,12]{2,0,1:T(2,128)} %param.15) | data formatting | bytes 1152 | tf_op args[2]
  1.3 0.0 copy-start
  1.3 0.9 %copy.19.grad_out = bf16[2,6,12,192]{3,2,1,0:T(8,128)(2,1)S(1)} copy(bf16[2,6,12,192]{3,0,2,1:T(2,128)(2,1)} %param.14) | data formatting | bytes 110592 | tf_op args[1]
  2.3 0.0 copy-start.3
  2.3 0.9 %copy.18.fields = bf16[2,6,12,192]{3,2,1,0:T(8,128)(2,1)S(1)} copy(bf16[2,6,12,192]{3,0,2,1:T(2,128)(2,1)} %param.13) | data formatting | bytes 110592 | tf_op args[0]
  3.2 0.0 copy-start.2
  3.2 0.0 copy-start.6
  3.2 0.0 copy-start.7
  3.3 0.0 copy-start.8
  3.3 1.0 %copy.21.table = f32[1,1,6,3312]{3,2,1,0:T(8,128)S(1)} copy(f32[1,1,6,3312]{3,1,2,0:T(1,128)} %param.19) | data formatting | bytes 158976 | tf_op args[6]
  4.2 0.0 copy-done
  4.2 0.0 copy-done.3
  4.2 0.0 copy-done.2
  4.3 0.0 copy-done.6
  4.3 0.0 copy-done.7
  4.3 0.0 copy-done.8
  4.3 0.0 copy-start.1
  4.3 1.0 %copy-done.1 = bf16[512,384]{1,0:T(8,128)(2,1)S(1)} copy-done((bf16[512,384]{1,0:T(8,128)(2,1)S(1)}, bf16[512,384]{1,0:T(8,128)(2,1)}, u32[]{:S(2)}) %copy-start.1) | copy-done | bytes 393240
  5.3 0.9 %copy-done.4 = bf16[192,192]{1,0:T(8,128)(2,1)S(1)} copy-done((bf16[192,192]{1,0:T(8,128)(2,1)S(1)}, bf16[192,192]{1,0:T(8,128)(2,1)}, u32[]{:S(2)}) %copy-start.4) | copy-done | bytes 73752
  6.2 0.9 %copy-done.5 = bf16[192,144]{1,0:T(8,128)(2,1)S(1)} copy-done((bf16[192,144]{1,0:T(8,128)(2,1)S(1)}, bf16[192,144]{1,0:T(8,128)(2,1)}, u32[]{:S(2)}) %copy-start.5) | copy-done | bytes 55320
  7.1 51.7 %shard_map.164 = (bf16[1152,128]{1,0:T(8,128)(2,1)S(1)}, bf16[192,192]{1,0:T(8,128)(2,1)S(1)}, bf16[256,128]{1,0:T(8,128)(2,1)S(1)}) custom-call(bf16[2,6,12,192]{3,2,1,0:T(8,128)(2,1)S(1)} %copy.18.fields, bf16[2,6,12,192]{3,2,1,0:T(8,128)(2,1)S(1)} %copy.19.grad_out, s32[2,6,12]{2,1,0:T(8,128)S(1)} %copy.20.ids, f32[192]{0:T(256)S(1)} %copy-done.8, ...), custom_call_target="tpu_custom_call" | custom-call | tf_op jit(solution)/shard_map/pallas_call | solution.py:483
  58.8 1.1 %shard_map.165 = (bf16[2,6,12,192]{3,2,1,0:T(8,128)(2,1)S(1)}, f32[192,576]{1,0:T(8,128)}, f32[192,192]{1,0:T(8,128)}, f32[192]{0:T(256)}, f32[1,1,6,3312]{3,2,1,0:T(8,128)S(1)}) custom-call(bf16[1152,128]{1,0:T(8,128)(2,1)S(1)} %get-tuple-element.8.flat, bf16[192,192]{1,0:T(8,128)(2,1)S(1)} %get-tuple-element.9.quads, ...), custom_call_target="tpu_custom_call" | custom-call | tf_op jit(solution)/shard_map/pallas_call | solution.py:498
  59.9 0.7 %copy.23 = bf16[2,6,12,192]{3,0,2,1:T(2,128)(2,1)} copy(bf16[2,6,12,192]{3,2,1,0:T(8,128)(2,1)S(1)} %get-tuple-element.11) | data formatting | bytes 110592 | tf_op jit(solution)/shard_map/pallas_call | solution.py:498
  60.6 0.7 %copy.24 = f32[1,1,6,3312]{3,1,2,0:T(1,128)} copy(f32[1,1,6,3312]{3,2,1,0:T(8,128)S(1)} %get-tuple-element.15) | data formatting | bytes 158976 | tf_op jit(solution)/shard_map/pallas_call | solution.py:498
  (2 shorter events, 0.0 us)
Async XLA Ops:
  1.3 2.9 %copy-start = (bf16[192,576]{1,0:T(8,128)(2,1)S(1)}, bf16[192,576]{1,0:T(8,128)(2,1)}, u32[]{:S(2)}) copy-start(bf16[192,576]{1,0:T(8,128)(2,1)} %wqkv.3) | copy-start | bytes 663556
  2.3 2.0 %copy-start.3 = (bf16[144,384]{1,0:T(8,128)(2,1)S(1)}, bf16[144,384]{1,0:T(8,128)(2,1)}, u32[]{:S(2)}) copy-start(bf16[144,384]{1,0:T(8,128)(2,1)} %constant.12.clone.gather) | copy-start | bytes 331780
  3.2 1.0 %copy-start.2 = (bf16[192,192]{1,0:T(8,128)(2,1)S(1)}, bf16[192,192]{1,0:T(8,128)(2,1)}, u32[]{:S(2)}) copy-start(bf16[192,192]{1,0:T(8,128)(2,1)} %constant.14.clone.place) | copy-start | bytes 221188
  3.2 1.0 %copy-start.6 = (bf16[144,128]{1,0:T(8,128)(2,1)S(1)}, bf16[144,128]{1,0:T(8,128)(2,1)}, u32[]{:S(2)}) copy-start(bf16[144,128]{1,0:T(8,128)(2,1)} %constant.17.clone.lon_of) | copy-start | bytes 110596
  3.2 1.0 %copy-start.7 = (bf16[144,16]{1,0:T(8,128)(2,1)S(1)}, bf16[144,16]{1,0:T(8,128)(2,1)}, u32[]{:S(2)}) copy-start(bf16[144,16]{1,0:T(8,128)(2,1)} %constant.16.clone.row_of) | copy-start | bytes 13828
  3.3 1.0 %copy-start.8 = (f32[192]{0:T(256)S(1)}, f32[192]{0:T(256)}, u32[]{:S(2)}) copy-start(f32[192]{0:T(256)} %gain.3) | copy-start | bytes 2308
  4.3 1.0 %copy-start.1 = (bf16[512,384]{1,0:T(8,128)(2,1)S(1)}, bf16[512,384]{1,0:T(8,128)(2,1)}, u32[]{:S(2)}) copy-start(bf16[512,384]{1,0:T(8,128)(2,1)} %constant.15.clone.shear) | copy-start | bytes 1179652
  5.3 0.9 %copy-start.4 = (bf16[192,192]{1,0:T(8,128)(2,1)S(1)}, bf16[192,192]{1,0:T(8,128)(2,1)}, u32[]{:S(2)}) copy-start(bf16[192,192]{1,0:T(8,128)(2,1)} %wproj.1) | copy-start | bytes 221188
  6.2 0.9 %copy-start.5 = (bf16[192,144]{1,0:T(8,128)(2,1)S(1)}, bf16[192,144]{1,0:T(8,128)(2,1)}, u32[]{:S(2)}) copy-start(bf16[192,144]{1,0:T(8,128)(2,1)} %constant.13.clone.scatter) | copy-start | bytes 165892

commit v2 on v1

v2 whole, which is shorter than its diff:
```python
import functools

import jax
import jax.numpy as jnp
import numpy as np
from jax import lax
from jax.experimental import pallas as pl
from jax.experimental.pallas import tpu as pltpu
from jax.sharding import PartitionSpec as P

D = 192
HEADS = 6
LON = 12
CELLS = 12
TOK = 144
SPAN = 23 * CELLS
SEG = 138
EPS = 1e-05
MESH = pl.DeviceIdType.MESH
BF = jnp.bfloat16
F32 = jnp.float32

INSIDE, ACROSS, FOUR = 16, 16, 4
ROWS = 1152 // (2 * INSIDE)
VMEM_LIMIT = 60 * 1024 * 1024


def token_tables():
    gather = np.zeros((TOK, TOK), np.float32)
    for o in range(12):
        for z in range(2):
            for a in range(6):
                s = (a >= 3) * 2 + (o >= 6)
                gather[o * 12 + z * 6 + a, ((s * 3 + a % 3) * 6 + o % 6) * 2 + (z + 1) % 2] = 1
    shear = np.zeros((512, 384), np.float32)
    for zq in range(2):
        for aq in range(6):
            for r in range(23):
                shear[zq * 256 + aq * 23 + r, r * 12 + zq * 6 + aq] = 1
    row_of = np.zeros((TOK, 16), np.float32)
    lon_of = np.zeros((TOK, 128), np.float32)
    for t in range(TOK):
        row_of[t, t % 12] = 1
        lon_of[t, t // 12] = 1
    return gather, shear, row_of, lon_of


def dot(a, b):
    return lax.dot_general(a, b, (((1,), (0,)), ((), ())), preferred_element_type=F32)


def dot_rows(a, b):
    return lax.dot_general(a, b, (((1,), (1,)), ((), ())), preferred_element_type=F32)


def dot_cols(a, b):
    return lax.dot_general(a, b, (((0,), (0,)), ((), ())), preferred_element_type=F32)


def split(v):
    hi = v.astype(BF)
    return hi, (v - hi.astype(F32)).astype(BF)


def expand_bias(table, shear, xs, bias):
    for zp in range(2):
        for zq in range(2):
            for ap in range(6):
                start = ((zp * 2 + zq) * 6 + ap) * SEG
                rows = pl.ds(zp * 6 + ap, HEADS, stride=CELLS)
                part = table[:, 0, start : start + SEG]
                rest = jnp.concatenate([part[:, 128:], jnp.zeros((HEADS, 256 - SEG), F32)], axis=1)
                xs[2 * zq, rows, :] = part[:, 0:128]
                xs[2 * zq + 1, rows, :] = rest
    hi, lo = split(jnp.concatenate([xs[k] for k in range(4)], axis=1))
    sheared = dot(hi, shear[...]) + dot(lo, shear[...])
    for op in range(LON):
        window = sheared[:, (11 - op) * 12 : (11 - op) * 12 + TOK]
        for h in range(HEADS):
            bias[h, op * 12 : (op + 1) * 12, :] = window[h * 12 : (h + 1) * 12]


def fold_bias(gs, shear, stacked, xs, flat):
    for op in range(LON):
        for h in range(HEADS):
            stacked[op, h * 12 : (h + 1) * 12, :] = gs[h, op * 12 : (op + 1) * 12, :]
    total = None
    for op in range(LON):
        left = (11 - op) * 12
        parts = [stacked[op]]
        if left:
            parts.insert(0, jnp.zeros((72, left), F32))
        if SPAN - left - TOK:
            parts.append(jnp.zeros((72, SPAN - left - TOK), F32))
        piece = jnp.concatenate(parts, axis=1) if len(parts) > 1 else parts[0]
        total = piece if total is None else total + piece
    total = jnp.concatenate([total, jnp.zeros((72, 384 - SPAN), F32)], axis=1)
    hi, lo = split(total)
    spread = dot_rows(hi, shear[...]) + dot_rows(lo, shear[...])
    for k in range(4):
        xs[k] = spread[:, 128 * k : 128 * k + 128]
    for zp in range(2):
        for zq in range(2):
            for ap in range(6):
                start = ((zp * 2 + zq) * 6 + ap) * SEG
                rows = pl.ds(zp * 6 + ap, HEADS, stride=CELLS)
                flat[0:HEADS, start : start + 128] = xs[2 * zq, rows, :]
                flat[0:HEADS, start + 128 : start + SEG] = xs[2 * zq + 1, rows, :][:, 0 : SEG - 128]


def window_ids(ids, row_of, lon_of, ms):
    ms[...] = jnp.zeros_like(ms)
    for a in range(6):
        ms[a : a + 1, 0:12] = ids[a, 0:1].astype(F32)
        ms[a + 6 : a + 7, 0:12] = ids[a, 1:2].astype(F32)
    m = ms[...].astype(BF)
    column = jnp.sum(dot(row_of[...], m) * lon_of[...].astype(F32), axis=1, keepdims=True)
    spread = dot_cols(m, row_of[...].astype(F32).T.astype(BF))
    row = jnp.sum(spread * lon_of[...].astype(F32).T, axis=0, keepdims=True)
    return column, row


def window_grads(x, g, same, gain, wqkv, wproj, bias, gs_out):
    x = x.astype(F32)
    centred = x - jnp.mean(x, axis=-1, keepdims=True)
    inv_std = lax.rsqrt(jnp.mean(centred * centred, axis=-1, keepdims=True) + EPS)
    normed = centred * inv_std
    hidden = (normed * gain).astype(BF)
    projected = dot(hidden, wqkv)
    scaling = 32 ** (-0.5)
    query = (projected[:, :D] * scaling).astype(BF)
    key = projected[:, D : 2 * D].astype(BF)
    value = projected[:, 2 * D :].astype(BF)
    grad_att = dot_rows(g, wproj).astype(BF)
    lane = lax.broadcasted_iota(jnp.int32, (TOK, D), 1) // 32
    zero = jnp.zeros((TOK, D), BF)
    attended = dv = dq = dk = None

    def add(total, term):
        return term if total is None else total + term

    for h in range(HEADS):
        mine = lane == h
        qh = jnp.where(mine, query, zero)
        kh = jnp.where(mine, key, zero)
        vh = jnp.where(mine, value, zero)
        gh = jnp.where(mine, grad_att, zero)
        scores = jnp.where(same, dot_rows(qh, key) + bias[h], -1000000000.0)
        raised = jnp.exp(scores - jnp.max(scores, axis=-1, keepdims=True))
        prob = raised * (1.0 / jnp.sum(raised, axis=-1, keepdims=True))
        prob_bf = prob.astype(BF)
        attended = add(attended, dot(prob_bf, vh))
        grad_prob = dot_rows(gh, value)
        dv = add(dv, dot_cols(prob_bf, gh))
        weighted = prob * grad_prob
        gs = weighted - prob * jnp.sum(weighted, axis=-1, keepdims=True)
        gs_out[h] = gs
        gs = gs.astype(BF)
        dq = add(dq, dot(gs, kh))
        dk = add(dk, dot_cols(gs, qh))
    joint = jnp.concatenate(
        [(dq * scaling).astype(BF), dk.astype(BF), dv.astype(BF)], axis=1
    )
    grad_qkv = dot_cols(hidden, joint)
    grad_proj = dot_cols(attended.astype(BF), g)

    def local():
        grad_hidden = dot_rows(joint, wqkv)
        scaled = grad_hidden * gain
        return (
            inv_std
            * (
                scaled
                - jnp.mean(scaled, axis=-1, keepdims=True)
                - normed * jnp.mean(scaled * normed, axis=-1, keepdims=True)
            )
        ).astype(BF)

    return grad_qkv, grad_proj, local


def pack_weights(grad_qkv, grad_proj, flat, out):
    for c in range(4):
        flat[c * 192 : (c + 1) * 192, :] = grad_qkv[:, c * 128 : (c + 1) * 128]
    flat[768:960, :] = jnp.concatenate([grad_qkv[:, 512:576], grad_proj[:, 128:192]], axis=1)
    flat[960:1152, :] = grad_proj[:, 0:128]
    for r in range(2 * INSIDE):
        out[r // INSIDE, r % INSIDE] = flat[ROWS * r : ROWS * (r + 1), :].astype(BF)


def finish_weights(rows, wqkv, gain, flat, out_qkv, out_proj, out_gain):
    for r in range(2 * INSIDE):
        flat[ROWS * r : ROWS * (r + 1), :] = rows[r // INSIDE, r % INSIDE].astype(F32)
    for c in range(4):
        out_qkv[:, c * 128 : (c + 1) * 128] = flat[c * 192 : (c + 1) * 192, :]
    last = flat[768:960, :]
    out_qkv[:, 512:576] = last[:, 0:64]
    out_proj[:, 128:192] = last[:, 64:128]
    out_proj[:, 0:128] = flat[960:1152, :]
    products = out_qkv[...] * wqkv[...].astype(F32)
    hi, lo = split(products)
    ones = jnp.ones((8, 576), BF)
    row = (dot_rows(ones, hi) + dot_rows(ones, lo))[0:1]
    out_gain[...] = (row / gain[...].reshape(1, D)).reshape(D)


def finish_fields(quads, grad_out, out):
    for s in range(4):
        rows = slice(0, 3) if s >= 2 else slice(3, 6)
        cols = slice(0, 6) if s % 2 else slice(6, 12)
        out[rows, cols] = (grad_out[rows, cols].astype(F32) + quads[s].astype(F32)).astype(BF)


def finish_table(rows, out):
    for k in range(26):
        width = min(128, 3312 - 128 * k)
        block = rows[k // 2].astype(F32)[8 * (k % 2) : 8 * (k % 2) + 8]
        for h in range(HEADS):
            out[h, :, 128 * k : 128 * k + width] = block[h : h + 1, 0:width]


def exchange(src_of, recv, group, sends, recvs):
    size, rank, device_of = group
    copies = []
    for k in range(1, size):
        peer = lax.rem(rank + k, size)
        copy = pltpu.make_async_remote_copy(
            src_ref=src_of(peer),
            dst_ref=recv.at[rank],
            send_sem=sends.at[k],
            recv_sem=recvs.at[k],
            device_id=device_of(peer),
            device_id_type=MESH,
        )
        copy.start()
        copies.append(copy)
    return copies


def arrive(copies):
    for copy in copies:
        copy.wait_recv()


def total_of(recv):
    total = recv[0].astype(F32)
    for k in range(1, recv.shape[0]):
        total = total + recv[k].astype(F32)
    return total


def kernel(
    fields, grad_out, ids_hbm, gain_hbm, wqkv_hbm, wproj_hbm, table_hbm,
    gather_hbm, shear_hbm, row_hbm, lon_hbm,
    out_flat, out_quads, out_table,
    ids, gain, wqkv, wproj, table, gather, shear, row_of, lon_of,
    field_in, grad_in, xs, bias, gs, stacked, ms, tflat, quads_out, quads_in,
    flat, w_out, w_in, w_half, w1, w2_out, w2, w3, t_out, t1, t2_out, t2, t3,
    block_sem, across_sem, load_sem, own_sem, halo_send, halo_recv, back_send, back_recv,
    pair_send, pair_recv, w1_send, w1_recv, w2_send, w2_recv, w3_send, w3_recv, w4_send, w4_recv,
    t1_send, t1_recv, t2_send, t2_recv, t3_send, t3_recv,
):
    l, a = lax.axis_index("lon"), lax.axis_index("lat")
    part, block = lax.rem(l, FOUR), l // FOUR
    core, side = lax.rem(part, 2), part // 2
    near_l, far_l = lax.rem(l + 63, 64), lax.rem(l + 1, 64)
    near_a, far_a = lax.rem(a + 7, 8), lax.rem(a + 1, 8)

    inside = (INSIDE, a * 2 + side, lambda r: (block * FOUR + lax.rem(r, 2) * 2 + core, r // 2))
    across = (ACROSS, block, lambda r: (r * FOUR + part, a))
    in_four = (FOUR, part, lambda r: (block * FOUR + r, a))
    barrier = pltpu.get_barrier_semaphore()
    near = ((near_l, a), (l, near_a), (near_l, near_a))
    far = ((far_l, a), (l, far_a), (far_l, far_a))
    beside = [(near_l, a), (far_l, a), near[2], far[2]]
    column = [(l, lax.rem(a + k, 8)) for k in range(1, 8)]
    four = [(block * FOUR + lax.rem(part + k, FOUR), a) for k in range(1, FOUR)]
    high, low = block // 4, lax.rem(block, 4)
    lows = [((high * 4 + lax.rem(low + k, 4)) * FOUR + part, a) for k in range(1, 4)]
    highs = [((lax.rem(high + k, 4) * 4 + low) * FOUR + part, a) for k in range(1, 4)]
    entry = beside + column + four + lows + highs
    for device in entry:
        pl.semaphore_signal(barrier, inc=1, device_id=device, device_id_type=MESH)
    loads = []
    pairs = (
        (table_hbm, table), (shear_hbm, shear), (ids_hbm, ids), (row_hbm, row_of), (lon_hbm, lon_of),
        (gather_hbm, gather), (gain_hbm, gain), (wqkv_hbm, wqkv), (wproj_hbm, wproj),
    )
    for k, (src, dst) in enumerate(pairs):
        load = pltpu.make_async_copy(src, dst, load_sem.at[k])
        load.start()
        loads.append(load)
    owns = []
    for k, (src, dst) in enumerate(((fields, field_in), (grad_out, grad_in))):
        own = pltpu.make_async_copy(src.at[3:6, 6:12], dst.at[0], own_sem.at[k])
        own.start()
        owns.append(own)
    pl.semaphore_wait(barrier, len(entry))

    halo = []
    for s in range(1, 4):
        rows = slice(0, 3) if s >= 2 else slice(3, 6)
        cols = slice(0, 6) if s % 2 else slice(6, 12)
        for k, (src, dst) in enumerate(((fields, field_in), (grad_out, grad_in))):
            copy = pltpu.make_async_remote_copy(
                src_ref=src.at[rows, cols],
                dst_ref=dst.at[s],
                send_sem=halo_send.at[2 * s + k],
                recv_sem=halo_recv.at[2 * s + k],
                device_id=near[s - 1],
                device_id_type=MESH,
            )
            copy.start()
            halo.append(copy)

    for device in four:
        pl.semaphore_signal(block_sem, inc=1, device_id=device, device_id_type=MESH)
    for device in highs:
        pl.semaphore_signal(across_sem, inc=1, device_id=device, device_id_type=MESH)

    for load in loads:
        load.wait()
    expand_bias(table, shear, xs, bias)
    ids_p, ids_q = window_ids(ids, row_of, lon_of, ms)
    same = ids_p == ids_q

    for own in owns:
        own.wait()
    arrive(halo)
    moved = dot(gather[...], field_in[...].reshape(TOK, D)).astype(BF)
    moved_grad = dot(gather[...], grad_in[...].reshape(TOK, D)).astype(BF)
    grad_qkv, grad_proj, local = window_grads(
        moved, moved_grad, same, gain[...].reshape(1, D), wqkv[...], wproj[...], bias, gs
    )

    pack_weights(grad_qkv, grad_proj, flat, w_out)
    rank = inside[1]
    pl.semaphore_wait(block_sem, FOUR - 1)
    pl.semaphore_wait(across_sem, 3)
    partner = (l + 1 - 2 * core, a)
    pair = []
    for k in range(4):
        copy = pltpu.make_async_remote_copy(
            src_ref=w_out.at[1 - core, 4 * k : 4 * k + 4],
            dst_ref=w_in.at[4 * k : 4 * k + 4],
            send_sem=pair_send.at[k],
            recv_sem=pair_recv.at[k],
            device_id=partner,
            device_id_type=MESH,
        )
        copy.start()
        pair.append(copy)

    tflat[...] = jnp.zeros_like(tflat)
    fold_bias(gs, shear, stacked, xs, tflat)
    for r in range(ACROSS):
        if r < 13:
            two = [tflat[:, 256 * r : 256 * r + 128], tflat[:, 256 * r + 128 : 256 * r + 256]]
            t_out[r] = jnp.concatenate(two, axis=0).astype(BF)
        else:
            t_out[r] = jnp.zeros((16, 128), BF)
    d1 = exchange(lambda r: t_out.at[r], t1, across, t1_send, t1_recv)
    t1[block] = t_out[block]

    arrive(pair)
    w_half[...] = (w_out[core].astype(F32) + w_in[...].astype(F32)).astype(BF)
    c1 = exchange(lambda r: w_half.at[r], w1, inside, w1_send, w1_recv)
    w1[rank] = w_half[rank]

    quads = dot_cols(gather[...], local()).astype(BF)
    quads_out[...] = quads.reshape(4, 3, 6, 2, D)
    back = []
    for s in range(1, 4):
        copy = pltpu.make_async_remote_copy(
            src_ref=quads_out.at[s],
            dst_ref=quads_in.at[s],
            send_sem=back_send.at[s],
            recv_sem=back_recv.at[s],
            device_id=far[s - 1],
            device_id_type=MESH,
        )
        copy.start()
        back.append(copy)
    quads_in[0] = quads_out[0]

    arrive(d1)
    mine = total_of(t1).astype(BF)
    t2_out[...] = mine
    t2[part] = mine
    d2 = exchange(lambda r: t2_out, t2, in_four, t2_send, t2_recv)

    arrive(c1)
    mine = total_of(w1).astype(BF)
    w2_out[...] = mine
    w2[block] = mine
    c2 = exchange(lambda r: w2_out, w2, across, w2_send, w2_recv)

    arrive(d2)
    t3[block] = total_of(t2).astype(BF)
    d3 = exchange(lambda r: t3.at[block], t3, across, t3_send, t3_recv)

    arrive(c2)
    w3[core, rank] = total_of(w2).astype(BF)
    c3 = exchange(lambda r: w3.at[core, rank], w3.at[core], inside, w3_send, w3_recv)

    arrive(back)
    out_quads[...] = quads_in[...]
    arrive(d3)
    out_table[...] = t3[...]
    c4 = []
    for k in range(INSIDE):
        if k:
            c3[k - 1].wait_recv()
        slot = lax.rem(rank + INSIDE - k, INSIDE)
        copy = pltpu.make_async_remote_copy(
            src_ref=w3.at[core, slot],
            dst_ref=w3.at[core, slot],
            send_sem=w4_send.at[k],
            recv_sem=w4_recv.at[k],
            device_id=partner,
            device_id_type=MESH,
        )
        copy.start()
        c4.append(copy)
    arrive(c4)
    out_flat[...] = w3[...]
    for copy in halo + back + pair + c1 + d1 + c2 + d2 + c3 + d3 + c4:
        copy.wait_send()


def finish(rows, quads, trows, grad_out, wqkv, gain, out_f, out_qkv, out_proj, out_gain, out_t, flat):
    finish_weights(rows, wqkv, gain, flat, out_qkv, out_proj, out_gain)
    finish_fields(quads, grad_out, out_f)
    finish_table(trows, out_t)


def body(fields, grad_out, mask_ids, ln_gain, qkv_weight, proj_weight, bias_table):
    consts = [jnp.asarray(v, BF) for v in token_tables()]
    fields = jnp.transpose(fields, (1, 2, 0, 3))
    grad_out = jnp.transpose(grad_out, (1, 2, 0, 3))
    vmem = pl.BlockSpec(memory_space=pltpu.VMEM)
    hbm = pl.BlockSpec(memory_space=pl.ANY)
    dma = pltpu.SemaphoreType.DMA
    scratch = [
        pltpu.VMEM((6, 2, 12), jnp.int32),
        pltpu.VMEM((D,), F32),
        pltpu.VMEM((D, 576), BF),
        pltpu.VMEM((D, D), BF),
        pltpu.VMEM((HEADS, 1, 3312), F32),
        pltpu.VMEM((TOK, TOK), BF),
        pltpu.VMEM((512, 384), BF),
        pltpu.VMEM((TOK, 16), BF),
        pltpu.VMEM((TOK, 128), BF),
        pltpu.VMEM((4, 3, 6, 2, D), BF),
        pltpu.VMEM((4, 3, 6, 2, D), BF),
        pltpu.VMEM((4, 72, 128), F32),
        pltpu.VMEM((HEADS, TOK, TOK), F32),
        pltpu.VMEM((HEADS, TOK, TOK), F32),
        pltpu.VMEM((LON, 72, TOK), F32),
        pltpu.VMEM((16, 128), F32),
        pltpu.VMEM((8, 3328), F32),
        pltpu.VMEM((4, 3, 6, 2, D), BF),
        pltpu.VMEM((4, 3, 6, 2, D), BF),
        pltpu.VMEM((1152, 128), F32),
        pltpu.VMEM((2, INSIDE, ROWS, 128), BF),
        pltpu.VMEM((INSIDE, ROWS, 128), BF),
        pltpu.VMEM((INSIDE, ROWS, 128), BF),
        pltpu.VMEM((INSIDE, ROWS, 128), BF),
        pltpu.VMEM((ROWS, 128), BF),
        pltpu.VMEM((ACROSS, ROWS, 128), BF),
        pltpu.VMEM((2, INSIDE, ROWS, 128), BF),
        pltpu.VMEM((ACROSS, 16, 128), BF),
        pltpu.VMEM((ACROSS, 16, 128), BF),
        pltpu.VMEM((16, 128), BF),
        pltpu.VMEM((FOUR, 16, 128), BF),
        pltpu.VMEM((ACROSS, 16, 128), BF),
        pltpu.SemaphoreType.REGULAR,
        pltpu.SemaphoreType.REGULAR,
        dma((9,)),
        dma((2,)),
        dma((8,)),
        dma((8,)),
        dma((4,)),
        dma((4,)),
        dma((4,)),
        dma((4,)),
        dma((INSIDE,)),
        dma((INSIDE,)),
        dma((ACROSS,)),
        dma((ACROSS,)),
        dma((INSIDE,)),
        dma((INSIDE,)),
        dma((INSIDE,)),
        dma((INSIDE,)),
        dma((ACROSS,)),
        dma((ACROSS,)),
        dma((FOUR,)),
        dma((FOUR,)),
        dma((ACROSS,)),
        dma((ACROSS,)),
    ]
    rows, quads, trows = pl.pallas_call(
        kernel,
        out_shape=(
            jax.ShapeDtypeStruct((2, INSIDE, ROWS, 128), BF),
            jax.ShapeDtypeStruct((4, 3, 6, 2, D), BF),
            jax.ShapeDtypeStruct((ACROSS, 16, 128), BF),
        ),
        in_specs=[hbm] * 11,
        out_specs=(vmem, vmem, vmem),
        scratch_shapes=scratch,
        compiler_params=pltpu.CompilerParams(
            collective_id=0, has_side_effects=True, vmem_limit_bytes=VMEM_LIMIT
        ),
    )(
        fields, grad_out, jnp.transpose(mask_ids, (1, 0, 2)), ln_gain, qkv_weight, proj_weight,
        bias_table.reshape(HEADS, 1, 3312), *consts,
    )
    out_f, out_qkv, out_proj, out_gain, out_t = pl.pallas_call(
        finish,
        out_shape=(
            jax.ShapeDtypeStruct((6, 12, 2, D), BF),
            jax.ShapeDtypeStruct((D, 576), F32),
            jax.ShapeDtypeStruct((D, D), F32),
            jax.ShapeDtypeStruct((D,), F32),
            jax.ShapeDtypeStruct((HEADS, 1, 3312), F32),
        ),
        in_specs=[vmem] * 6,
        out_specs=(vmem,) * 5,
        scratch_shapes=[pltpu.VMEM((1152, 128), F32)],
        compiler_params=pltpu.CompilerParams(vmem_limit_bytes=VMEM_LIMIT),
    )(rows, quads, trows, grad_out, qkv_weight, ln_gain)
    out_f = jnp.transpose(out_f, (2, 0, 1, 3))
    return out_f, out_qkv, out_proj, out_gain, out_t.reshape(1, 1, HEADS, 3312)


def solution(mesh):
    placed = (
        P(None, "lat", "lon", None),
        P(None, "lat", "lon", None),
        P(None, "lat", "lon"),
        P(),
        P(),
        P(),
        P("lat", None, None, None),
    )
    return jax.shard_map(
        body,
        mesh=mesh,
        in_specs=placed,
        out_specs=(P(None, "lat", "lon", None), P(), P(), P(), P("lat", None, None, None)),
        check_vma=False,
    )
```

time: 61.7 us -> 51.1 us (0.83)
  local copies, waits for them, and re-layouts: 7.76 us -> 0 us
  Pallas kernels: 52.8 us -> 50.3 us
    unnamed x22 -> x0, local copies, waits for them, and re-layouts: 6.33 us -> none
    pallas_call x2, Pallas kernels: 52.8 us -> 50.3 us  [the longest x1 48.1 us: body(): pl.pallas_call(kernel, out_shape=(jax.ShapeDtypeStruct((2, INSIDE, ROWS,...]
    pallas_call x2 -> x0, local copies, waits for them, and re-layouts: 1.43 us -> none  [body(): pl.pallas_call(finish, out_shape=(jax.ShapeDtypeStruct((2, 6, 12, D), BF)...]
where the time goes in v2:
time: 51.1 us; the launch traced here: 51 us
  Pallas kernels  50.3 us (98%)
  between operations  0.64 us (1%)
    pallas_call x1, Pallas kernels, body(): pl.pallas_call(kernel, out_shape=(jax.ShapeDtypeStruct((2, INSIDE, ROWS,...  48.1 us
    pallas_call x1, Pallas kernels, body(): pl.pallas_call(finish, out_shape=(jax.ShapeDtypeStruct((6, 12, 2, D), BF)...  2.2 us

profile of v2, /device:TPU:1, one launch (start us, length us, event | category | flops | bytes accessed | tf_op | source)
XLA Modules:
  0.0 51.0 jit_solution(1170849772060421632)
XLA Ops:
  0.6 48.1 %shard_map.146 = (bf16[2,16,36,128]{3,2,1,0:T(8,128)(2,1)}, bf16[4,3,6,2,192]{4,3,2,1,0:T(2,128)(2,1)}, bf16[16,16,128]{2,1,0:T(8,128)(2,1)}) custom-call(bf16[6,12,2,192]{3,2,1,0:T(2,128)(2,1)} %bitcast.11, bf16[6,12,2,192]{3,2,1,0:T(2,128)(2,1)} %bitcast.8, s32[6,2,12]{2,1,0:T(2,128)} %bitcast.12, f32[192]{0:T(256)} %gain.1, bf16[192,576]{1,0:T(8,128)(2,1)} %wqkv.1, ...), custom_call_target="tpu_custom_call" | custom-call | tf_op jit(solution)/shard_map/pallas_call | solution.py:502
  48.8 2.2 %shard_map.147 = (bf16[6,12,2,192]{3,2,1,0:T(2,128)(2,1)}, f32[192,576]{1,0:T(8,128)}, f32[192,192]{1,0:T(8,128)}, f32[192]{0:T(256)}, f32[6,1,3312]{2,1,0:T(1,128)}) custom-call(bf16[2,16,36,128]{3,2,1,0:T(8,128)(2,1)} %get-tuple-element.13.rows, bf16[4,3,6,2,192]{4,3,2,1,0:T(2,128)(2,1)} %get-tuple-element.14.quads, ...), custom_call_target="tpu_custom_call" | custom-call | tf_op jit(solution)/shard_map/pallas_call | solution.py:519

commit v3 on v2

--- a/solution.py
+++ b/solution.py
@@ -134,30 +134,39 @@
     grad_att = dot_rows(g, wproj).astype(BF)
     lane = lax.broadcasted_iota(jnp.int32, (TOK, D), 1) // 32
     zero = jnp.zeros((TOK, D), BF)
-    attended = dv = dq = dk = None
-
-    def add(total, term):
-        return term if total is None else total + term
-
-    for h in range(HEADS):
-        mine = lane == h
-        qh = jnp.where(mine, query, zero)
-        kh = jnp.where(mine, key, zero)
-        vh = jnp.where(mine, value, zero)
-        gh = jnp.where(mine, grad_att, zero)
-        scores = jnp.where(same, dot_rows(qh, key) + bias[h], -1000000000.0)
-        raised = jnp.exp(scores - jnp.max(scores, axis=-1, keepdims=True))
-        prob = raised * (1.0 / jnp.sum(raised, axis=-1, keepdims=True))
-        prob_bf = prob.astype(BF)
-        attended = add(attended, dot(prob_bf, vh))
-        grad_prob = dot_rows(gh, value)
-        dv = add(dv, dot_cols(prob_bf, gh))
-        weighted = prob * grad_prob
-        gs = weighted - prob * jnp.sum(weighted, axis=-1, keepdims=True)
-        gs_out[h] = gs
-        gs = gs.astype(BF)
-        dq = add(dq, dot(gs, kh))
-        dk = add(dk, dot_cols(gs, qh))
+    heads = range(HEADS)
+
+    def by_head(v):
+        return [jnp.where(lane == h, v, zero) for h in heads]
+
+    def stack(v):
+        return jnp.concatenate(v, axis=0)
+
+    def unstack(v):
+        return [v[h * TOK : (h + 1) * TOK] for h in heads]
+
+    def over_heads(left, right):
+        total = dot(left[0], right[0])
+        for h in range(1, HEADS):
+            total = total + dot(left[h], right[h])
+        return total
+
+    queries, grads = stack(by_head(query)), stack(by_head(grad_att))
+    scores = unstack(dot_rows(queries, key))
+    grad_prob = unstack(dot_rows(grads, value))
+    scores = [jnp.where(same, scores[h] + bias[h], -1000000000.0) for h in heads]
+    raised = [jnp.exp(v - jnp.max(v, axis=-1, keepdims=True)) for v in scores]
+    prob = [v * (1.0 / jnp.sum(v, axis=-1, keepdims=True)) for v in raised]
+    prob_bf = [v.astype(BF) for v in prob]
+    weighted = [prob[h] * grad_prob[h] for h in heads]
+    gs = [w - p * jnp.sum(w, axis=-1, keepdims=True) for w, p in zip(weighted, prob)]
+    for h in heads:
+        gs_out[h] = gs[h]
+    gs = [v.astype(BF) for v in gs]
+    attended = over_heads(prob_bf, by_head(value))
+    dv = dot_cols(stack(prob_bf), grads)
+    dq = over_heads(gs, by_head(key))
+    dk = dot_cols(stack(gs), queries)
     joint = jnp.concatenate(
         [(dq * scaling).astype(BF), dk.astype(BF), dv.astype(BF)], axis=1
     )
@@ -219,7 +228,7 @@
             out[h, :, 128 * k : 128 * k + width] = block[h : h + 1, 0:width]
 
 
-def exchange(src_of, recv, group, sends, recvs):
+def exchange(src_of, recv, group, send_sem, recv_sem):
     size, rank, device_of = group
     copies = []
     for k in range(1, size):
@@ -227,14 +236,18 @@
         copy = pltpu.make_async_remote_copy(
             src_ref=src_of(peer),
             dst_ref=recv.at[rank],
-            send_sem=sends.at[k],
-            recv_sem=recvs.at[k],
+            send_sem=send_sem,
+            recv_sem=recv_sem.at[k] if len(recv_sem.shape) else recv_sem,
             device_id=device_of(peer),
             device_id_type=MESH,
         )
         copy.start()
         copies.append(copy)
     return copies
+
+
+def wait_bytes(ref, sem):
+    pltpu.make_async_copy(ref, ref, sem).wait()
 
 
 def arrive(copies):
@@ -278,7 +291,7 @@
     high, low = block // 4, lax.rem(block, 4)
     lows = [((high * 4 + lax.rem(low + k, 4)) * FOUR + part, a) for k in range(1, 4)]
     highs = [((lax.rem(high + k, 4) * 4 + low) * FOUR + part, a) for k in range(1, 4)]
-    entry = beside + column + four + lows + highs
+    entry = highs + lows + column + beside + four
     for device in entry:
         pl.semaphore_signal(barrier, inc=1, device_id=device, device_id_type=MESH)
     loads = []
@@ -338,34 +351,14 @@
     pl.semaphore_wait(block_sem, FOUR - 1)
     pl.semaphore_wait(across_sem, 3)
     partner = (l + 1 - 2 * core, a)
-    pair = []
-    for k in range(4):
-        copy = pltpu.make_async_remote_copy(
-            src_ref=w_out.at[1 - core, 4 * k : 4 * k + 4],
-            dst_ref=w_in.at[4 * k : 4 * k + 4],
-            send_sem=pair_send.at[k],
-            recv_sem=pair_recv.at[k],
-            device_id=partner,
-            device_id_type=MESH,
-        )
-        copy.start()
-        pair.append(copy)
-
-    tflat[...] = jnp.zeros_like(tflat)
-    fold_bias(gs, shear, stacked, xs, tflat)
-    for r in range(ACROSS):
-        if r < 13:
-            two = [tflat[:, 256 * r : 256 * r + 128], tflat[:, 256 * r + 128 : 256 * r + 256]]
-            t_out[r] = jnp.concatenate(two, axis=0).astype(BF)
-        else:
-            t_out[r] = jnp.zeros((16, 128), BF)
-    d1 = exchange(lambda r: t_out.at[r], t1, across, t1_send, t1_recv)
-    t1[block] = t_out[block]
-
-    arrive(pair)
-    w_half[...] = (w_out[core].astype(F32) + w_in[...].astype(F32)).astype(BF)
-    c1 = exchange(lambda r: w_half.at[r], w1, inside, w1_send, w1_recv)
-    w1[rank] = w_half[rank]
+    pltpu.make_async_remote_copy(
+        src_ref=w_out.at[1 - core],
+        dst_ref=w_in,
+        send_sem=pair_send,
+        recv_sem=pair_recv,
+        device_id=partner,
+        device_id_type=MESH,
+    ).start()
 
     quads = dot_cols(gather[...], local()).astype(BF)
     quads_out[...] = quads.reshape(4, 3, 6, 2, D)
@@ -383,49 +376,72 @@
         back.append(copy)
     quads_in[0] = quads_out[0]
 
-    arrive(d1)
+    wait_bytes(w_in, pair_recv)
+    w_half[...] = (w_out[core].astype(F32) + w_in[...].astype(F32)).astype(BF)
+    exchange(lambda r: w_half.at[r], w1, inside, w1_send, w1_recv)
+    w1[rank] = w_half[rank]
+
+    tflat[...] = jnp.zeros_like(tflat)
+    fold_bias(gs, shear, stacked, xs, tflat)
+    for r in range(ACROSS):
+        if r < 13:
+            two = [tflat[:, 256 * r : 256 * r + 128], tflat[:, 256 * r + 128 : 256 * r + 256]]
+            t_out[r] = jnp.concatenate(two, axis=0).astype(BF)
+        else:
+            t_out[r] = jnp.zeros((16, 128), BF)
+    exchange(lambda r: t_out.at[r], t1, across, t1_send, t1_recv)
+    t1[block] = t_out[block]
+    for copy in halo:
+        copy.wait_send()
+    wait_bytes(w_in, pair_send)
+
+    wait_bytes(w1.at[1:], w1_recv)
+    mine = total_of(w1).astype(BF)
+    w2_out[...] = mine
+    w2[block] = mine
+    exchange(lambda r: w2_out, w2, across, w2_send, w2_recv)
+
+    wait_bytes(t1.at[1:], t1_recv)
     mine = total_of(t1).astype(BF)
     t2_out[...] = mine
     t2[part] = mine
-    d2 = exchange(lambda r: t2_out, t2, in_four, t2_send, t2_recv)
-
-    arrive(c1)
-    mine = total_of(w1).astype(BF)
-    w2_out[...] = mine
-    w2[block] = mine
-    c2 = exchange(lambda r: w2_out, w2, across, w2_send, w2_recv)
-
-    arrive(d2)
+    exchange(lambda r: t2_out, t2, in_four, t2_send, t2_recv)
+    wait_bytes(w1.at[1:], w1_send)
+    wait_bytes(t1.at[1:], t1_send)
+    arrive(back)
+    out_quads[...] = quads_in[...]
+
+    wait_bytes(t2.at[1:], t2_recv)
     t3[block] = total_of(t2).astype(BF)
-    d3 = exchange(lambda r: t3.at[block], t3, across, t3_send, t3_recv)
-
-    arrive(c2)
+    exchange(lambda r: t3.at[block], t3, across, t3_send, t3_recv)
+
+    wait_bytes(w2.at[1:], w2_recv)
     w3[core, rank] = total_of(w2).astype(BF)
     c3 = exchange(lambda r: w3.at[core, rank], w3.at[core], inside, w3_send, w3_recv)
-
-    arrive(back)
-    out_quads[...] = quads_in[...]
-    arrive(d3)
-    out_table[...] = t3[...]
-    c4 = []
+    for copy in back:
+        copy.wait_send()
+    wait_bytes(w2.at[1:], w2_send)
+    wait_bytes(t2.at[1:], t2_send)
+
     for k in range(INSIDE):
         if k:
             c3[k - 1].wait_recv()
         slot = lax.rem(rank + INSIDE - k, INSIDE)
-        copy = pltpu.make_async_remote_copy(
+        pltpu.make_async_remote_copy(
             src_ref=w3.at[core, slot],
             dst_ref=w3.at[core, slot],
-            send_sem=w4_send.at[k],
-            recv_sem=w4_recv.at[k],
+            send_sem=w4_send,
+            recv_sem=w4_recv,
             device_id=partner,
             device_id_type=MESH,
-        )
-        copy.start()
-        c4.append(copy)
-    arrive(c4)
+        ).start()
+    wait_bytes(t3.at[1:], t3_recv)
+    out_table[...] = t3[...]
+    wait_bytes(t3.at[1:], t3_send)
+    wait_bytes(w1.at[1:], w3_send)
+    wait_bytes(w1, w4_recv)
     out_flat[...] = w3[...]
-    for copy in halo + back + pair + c1 + d1 + c2 + d2 + c3 + d3 + c4:
-        copy.wait_send()
+    wait_bytes(w1, w4_send)
 
 
 def finish(rows, quads, trows, grad_out, wqkv, gain, out_f, out_qkv, out_proj, out_gain, out_t, flat):
@@ -482,22 +498,9 @@
         dma((8,)),
         dma((4,)),
         dma((4,)),
-        dma((4,)),
-        dma((4,)),
+        *([dma] * 7),
         dma((INSIDE,)),
-        dma((INSIDE,)),
-        dma((ACROSS,)),
-        dma((ACROSS,)),
-        dma((INSIDE,)),
-        dma((INSIDE,)),
-        dma((INSIDE,)),
-        dma((INSIDE,)),
-        dma((ACROSS,)),
-        dma((ACROSS,)),
-        dma((FOUR,)),
-        dma((FOUR,)),
-        dma((ACROSS,)),
-        dma((ACROSS,)),
+        *([dma] * 8),
     ]
     rows, quads, trows = pl.pallas_call(
         kernel,

time: 51.1 us -> 46.8 us (0.916)
  Pallas kernels: 50.3 us -> 46 us
    pallas_call x1, Pallas kernels: 48.1 us -> 43.8 us  [body(): pl.pallas_call(kernel, out_shape=(jax.ShapeDtypeStruct((2, INSIDE, ROWS,...]
where the time goes in v3:
time: 46.8 us; the launch traced here: 46.7 us
  Pallas kernels  46 us (98%)
  between operations  0.64 us (1%)
    pallas_call x1, Pallas kernels, body(): pl.pallas_call(kernel, out_shape=(jax.ShapeDtypeStruct((2, INSIDE, ROWS,...  43.8 us
    pallas_call x1, Pallas kernels, body(): pl.pallas_call(finish, out_shape=(jax.ShapeDtypeStruct((6, 12, 2, D), BF)...  2.2 us

profile of v3, /device:TPU:1, one launch (start us, length us, event | category | flops | bytes accessed | tf_op | source)
XLA Modules:
  0.0 46.7 jit_solution(7222403003866337051)
XLA Ops:
  0.6 43.8 %shard_map.146 = (bf16[2,16,36,128]{3,2,1,0:T(8,128)(2,1)}, bf16[4,3,6,2,192]{4,3,2,1,0:T(2,128)(2,1)}, bf16[16,16,128]{2,1,0:T(8,128)(2,1)}) custom-call(bf16[6,12,2,192]{3,2,1,0:T(2,128)(2,1)} %bitcast.11, bf16[6,12,2,192]{3,2,1,0:T(2,128)(2,1)} %bitcast.8, s32[6,2,12]{2,1,0:T(2,128)} %bitcast.12, f32[192]{0:T(256)} %gain.1, bf16[192,576]{1,0:T(8,128)(2,1)} %wqkv.1, ...), custom_call_target="tpu_custom_call" | custom-call | tf_op jit(solution)/shard_map/pallas_call | solution.py:505
  44.5 2.2 %shard_map.147 = (bf16[6,12,2,192]{3,2,1,0:T(2,128)(2,1)}, f32[192,576]{1,0:T(8,128)}, f32[192,192]{1,0:T(8,128)}, f32[192]{0:T(256)}, f32[6,1,3312]{2,1,0:T(1,128)}) custom-call(bf16[2,16,36,128]{3,2,1,0:T(8,128)(2,1)} %get-tuple-element.13.rows, bf16[4,3,6,2,192]{4,3,2,1,0:T(2,128)(2,1)} %get-tuple-element.14.quads, ...), custom_call_target="tpu_custom_call" | custom-call | tf_op jit(solution)/shard_map/pallas_call | solution.py:522

commit v4 on v3

--- a/solution.py
+++ b/solution.py
@@ -120,7 +120,7 @@
     return column, row
 
 
-def window_grads(x, g, same, gain, wqkv, wproj, bias, gs_out):
+def window_grads(x, g, gain, wqkv, wproj, bias, gs_out):
     x = x.astype(F32)
     centred = x - jnp.mean(x, axis=-1, keepdims=True)
     inv_std = lax.rsqrt(jnp.mean(centred * centred, axis=-1, keepdims=True) + EPS)
@@ -154,7 +154,7 @@
     queries, grads = stack(by_head(query)), stack(by_head(grad_att))
     scores = unstack(dot_rows(queries, key))
     grad_prob = unstack(dot_rows(grads, value))
-    scores = [jnp.where(same, scores[h] + bias[h], -1000000000.0) for h in heads]
+    scores = [scores[h] + bias[h] for h in heads]
     raised = [jnp.exp(v - jnp.max(v, axis=-1, keepdims=True)) for v in scores]
     prob = [v * (1.0 / jnp.sum(v, axis=-1, keepdims=True)) for v in raised]
     prob_bf = [v.astype(BF) for v in prob]
@@ -269,7 +269,7 @@
     ids, gain, wqkv, wproj, table, gather, shear, row_of, lon_of,
     field_in, grad_in, xs, bias, gs, stacked, ms, tflat, quads_out, quads_in,
     flat, w_out, w_in, w_half, w1, w2_out, w2, w3, t_out, t1, t2_out, t2, t3,
-    block_sem, across_sem, load_sem, own_sem, halo_send, halo_recv, back_send, back_recv,
+    block_sem, across_sem, out_sem, load_sem, own_sem, halo_send, halo_recv, back_send, back_recv,
     pair_send, pair_recv, w1_send, w1_recv, w2_send, w2_recv, w3_send, w3_recv, w4_send, w4_recv,
     t1_send, t1_recv, t2_send, t2_recv, t3_send, t3_recv,
 ):
@@ -336,6 +336,8 @@
     expand_bias(table, shear, xs, bias)
     ids_p, ids_q = window_ids(ids, row_of, lon_of, ms)
     same = ids_p == ids_q
+    for h in range(HEADS):
+        bias[h] = jnp.where(same, bias[h], -1000000000.0)
 
     for own in owns:
         own.wait()
@@ -343,7 +345,7 @@
     moved = dot(gather[...], field_in[...].reshape(TOK, D)).astype(BF)
     moved_grad = dot(gather[...], grad_in[...].reshape(TOK, D)).astype(BF)
     grad_qkv, grad_proj, local = window_grads(
-        moved, moved_grad, same, gain[...].reshape(1, D), wqkv[...], wproj[...], bias, gs
+        moved, moved_grad, gain[...].reshape(1, D), wqkv[...], wproj[...], bias, gs
     )
 
     pack_weights(grad_qkv, grad_proj, flat, w_out)
@@ -351,15 +353,47 @@
     pl.semaphore_wait(block_sem, FOUR - 1)
     pl.semaphore_wait(across_sem, 3)
     partner = (l + 1 - 2 * core, a)
-    pltpu.make_async_remote_copy(
-        src_ref=w_out.at[1 - core],
-        dst_ref=w_in,
-        send_sem=pair_send,
-        recv_sem=pair_recv,
-        device_id=partner,
-        device_id_type=MESH,
-    ).start()
-
+    pair = []
+    for k in range(1, INSIDE + 1):
+        slot = lax.rem(rank + k, INSIDE)
+        copy = pltpu.make_async_remote_copy(
+            src_ref=w_out.at[1 - core, slot],
+            dst_ref=w_in.at[slot],
+            send_sem=pair_send,
+            recv_sem=pair_recv.at[k - 1],
+            device_id=partner,
+            device_id_type=MESH,
+        )
+        copy.start()
+        pair.append(copy)
+
+    for k in range(1, INSIDE + 1):
+        slot = lax.rem(rank + k, INSIDE)
+        pair[k - 1].wait_recv()
+        both = (w_out[core, slot].astype(F32) + w_in[slot].astype(F32)).astype(BF)
+        if k == INSIDE:
+            w1[slot] = both
+        else:
+            w_half[slot] = both
+            pltpu.make_async_remote_copy(
+                src_ref=w_half.at[slot],
+                dst_ref=w1.at[rank],
+                send_sem=w1_send,
+                recv_sem=w1_recv,
+                device_id=inside[2](slot),
+                device_id_type=MESH,
+            ).start()
+
+    tflat[...] = jnp.zeros_like(tflat)
+    fold_bias(gs, shear, stacked, xs, tflat)
+    for r in range(ACROSS):
+        if r < 13:
+            two = [tflat[:, 256 * r : 256 * r + 128], tflat[:, 256 * r + 128 : 256 * r + 256]]
+            t_out[r] = jnp.concatenate(two, axis=0).astype(BF)
+        else:
+            t_out[r] = jnp.zeros((16, 128), BF)
+    exchange(lambda r: t_out.at[r], t1, across, t1_send, t1_recv)
+    t1[block] = t_out[block]
     quads = dot_cols(gather[...], local()).astype(BF)
     quads_out[...] = quads.reshape(4, 3, 6, 2, D)
     back = []
@@ -376,21 +410,6 @@
         back.append(copy)
     quads_in[0] = quads_out[0]
 
-    wait_bytes(w_in, pair_recv)
-    w_half[...] = (w_out[core].astype(F32) + w_in[...].astype(F32)).astype(BF)
-    exchange(lambda r: w_half.at[r], w1, inside, w1_send, w1_recv)
-    w1[rank] = w_half[rank]
-
-    tflat[...] = jnp.zeros_like(tflat)
-    fold_bias(gs, shear, stacked, xs, tflat)
-    for r in range(ACROSS):
-        if r < 13:
-            two = [tflat[:, 256 * r : 256 * r + 128], tflat[:, 256 * r + 128 : 256 * r + 256]]
-            t_out[r] = jnp.concatenate(two, axis=0).astype(BF)
-        else:
-            t_out[r] = jnp.zeros((16, 128), BF)
-    exchange(lambda r: t_out.at[r], t1, across, t1_send, t1_recv)
-    t1[block] = t_out[block]
     for copy in halo:
         copy.wait_send()
     wait_bytes(w_in, pair_send)
@@ -409,7 +428,8 @@
     wait_bytes(w1.at[1:], w1_send)
     wait_bytes(t1.at[1:], t1_send)
     arrive(back)
-    out_quads[...] = quads_in[...]
+    quads_done = pltpu.make_async_copy(quads_in, out_quads, out_sem.at[1])
+    quads_done.start()
 
     wait_bytes(t2.at[1:], t2_recv)
     t3[block] = total_of(t2).astype(BF)
@@ -429,19 +449,24 @@
         slot = lax.rem(rank + INSIDE - k, INSIDE)
         pltpu.make_async_remote_copy(
             src_ref=w3.at[core, slot],
-            dst_ref=w3.at[core, slot],
+            dst_ref=out_flat.at[core, slot],
             send_sem=w4_send,
             recv_sem=w4_recv,
             device_id=partner,
             device_id_type=MESH,
         ).start()
+    rows_out = pltpu.make_async_copy(w3.at[core], out_flat.at[core], out_sem.at[2])
+    rows_out.start()
     wait_bytes(t3.at[1:], t3_recv)
-    out_table[...] = t3[...]
+    table_out = pltpu.make_async_copy(t3, out_table, out_sem.at[0])
+    table_out.start()
     wait_bytes(t3.at[1:], t3_send)
     wait_bytes(w1.at[1:], w3_send)
     wait_bytes(w1, w4_recv)
-    out_flat[...] = w3[...]
     wait_bytes(w1, w4_send)
+    quads_done.wait()
+    table_out.wait()
+    rows_out.wait()
 
 
 def finish(rows, quads, trows, grad_out, wqkv, gain, out_f, out_qkv, out_proj, out_gain, out_t, flat):
@@ -492,13 +517,16 @@
         pltpu.VMEM((ACROSS, 16, 128), BF),
         pltpu.SemaphoreType.REGULAR,
         pltpu.SemaphoreType.REGULAR,
+        dma((3,)),
         dma((9,)),
         dma((2,)),
         dma((8,)),
         dma((8,)),
         dma((4,)),
         dma((4,)),
-        *([dma] * 7),
+        dma,
+        dma((INSIDE,)),
+        *([dma] * 5),
         dma((INSIDE,)),
         *([dma] * 8),
     ]
@@ -510,7 +538,7 @@
             jax.ShapeDtypeStruct((ACROSS, 16, 128), BF),
         ),
         in_specs=[hbm] * 11,
-        out_specs=(vmem, vmem, vmem),
+        out_specs=(hbm, hbm, hbm),
         scratch_shapes=scratch,
         compiler_params=pltpu.CompilerParams(
             collective_id=0, has_side_effects=True, vmem_limit_bytes=VMEM_LIMIT

time: 46.8 us -> 45.9 us (0.981)
  Pallas kernels: 46 us -> 45.1 us
    pallas_call x1, Pallas kernels: 43.8 us -> 42.9 us  [body(): pl.pallas_call(kernel, out_shape=(jax.ShapeDtypeStruct((2, INSIDE, ROWS,...]
where the time goes in v4:
time: 45.9 us; the launch traced here: 45.8 us
  Pallas kernels  45.1 us (98%)
  between operations  0.64 us (1%)
    pallas_call x1, Pallas kernels, body(): pl.pallas_call(kernel, out_shape=(jax.ShapeDtypeStruct((2, INSIDE, ROWS,...  42.9 us
    pallas_call x1, Pallas kernels, body(): pl.pallas_call(finish, out_shape=(jax.ShapeDtypeStruct((6, 12, 2, D), BF)...  2.2 us

profile of v4, /device:TPU:1, one launch (start us, length us, event | category | flops | bytes accessed | tf_op | source)
XLA Modules:
  0.0 45.8 jit_solution(11751232036117433860)
XLA Ops:
  0.6 42.9 %shard_map.146 = (bf16[2,16,36,128]{3,2,1,0:T(8,128)(2,1)}, bf16[4,3,6,2,192]{4,3,2,1,0:T(2,128)(2,1)}, bf16[16,16,128]{2,1,0:T(8,128)(2,1)}) custom-call(bf16[6,12,2,192]{3,2,1,0:T(2,128)(2,1)} %bitcast.11, bf16[6,12,2,192]{3,2,1,0:T(2,128)(2,1)} %bitcast.8, s32[6,2,12]{2,1,0:T(2,128)} %bitcast.12, f32[192]{0:T(256)} %gain.1, bf16[192,576]{1,0:T(8,128)(2,1)} %wqkv.1, ...), custom_call_target="tpu_custom_call" | custom-call | tf_op jit(solution)/shard_map/pallas_call | solution.py:533
  43.6 2.2 %shard_map.147 = (bf16[6,12,2,192]{3,2,1,0:T(2,128)(2,1)}, f32[192,576]{1,0:T(8,128)}, f32[192,192]{1,0:T(8,128)}, f32[192]{0:T(256)}, f32[6,1,3312]{2,1,0:T(1,128)}) custom-call(bf16[2,16,36,128]{3,2,1,0:T(8,128)(2,1)} %get-tuple-element.13.rows, bf16[4,3,6,2,192]{4,3,2,1,0:T(2,128)(2,1)} %get-tuple-element.14.quads, ...), custom_call_target="tpu_custom_call" | custom-call | tf_op jit(solution)/shard_map/pallas_call | solution.py:550

commit v5 on v4

--- a/solution.py
+++ b/solution.py
@@ -72,7 +72,7 @@
                 rest = jnp.concatenate([part[:, 128:], jnp.zeros((HEADS, 256 - SEG), F32)], axis=1)
                 xs[2 * zq, rows, :] = part[:, 0:128]
                 xs[2 * zq + 1, rows, :] = rest
-    hi, lo = split(jnp.concatenate([xs[k] for k in range(4)], axis=1))
+    hi, lo = split(jnp.concatenate([xs[k, 0:72] for k in range(4)], axis=1))
     sheared = dot(hi, shear[...]) + dot(lo, shear[...])
     for op in range(LON):
         window = sheared[:, (11 - op) * 12 : (11 - op) * 12 + TOK]
@@ -98,7 +98,7 @@
     hi, lo = split(total)
     spread = dot_rows(hi, shear[...]) + dot_rows(lo, shear[...])
     for k in range(4):
-        xs[k] = spread[:, 128 * k : 128 * k + 128]
+        xs[k, 0:72] = spread[:, 128 * k : 128 * k + 128]
     for zp in range(2):
         for zq in range(2):
             for ap in range(6):
@@ -310,7 +310,6 @@
         owns.append(own)
     pl.semaphore_wait(barrier, len(entry))
 
-    halo = []
     for s in range(1, 4):
         rows = slice(0, 3) if s >= 2 else slice(3, 6)
         cols = slice(0, 6) if s % 2 else slice(6, 12)
@@ -318,13 +317,12 @@
             copy = pltpu.make_async_remote_copy(
                 src_ref=src.at[rows, cols],
                 dst_ref=dst.at[s],
-                send_sem=halo_send.at[2 * s + k],
-                recv_sem=halo_recv.at[2 * s + k],
+                send_sem=halo_send.at[k],
+                recv_sem=halo_recv.at[k],
                 device_id=near[s - 1],
                 device_id_type=MESH,
             )
             copy.start()
-            halo.append(copy)
 
     for device in four:
         pl.semaphore_signal(block_sem, inc=1, device_id=device, device_id_type=MESH)
@@ -341,7 +339,8 @@
 
     for own in owns:
         own.wait()
-    arrive(halo)
+    wait_bytes(field_in.at[1:], halo_recv.at[0])
+    wait_bytes(grad_in.at[1:], halo_recv.at[1])
     moved = dot(gather[...], field_in[...].reshape(TOK, D)).astype(BF)
     moved_grad = dot(gather[...], grad_in[...].reshape(TOK, D)).astype(BF)
     grad_qkv, grad_proj, local = window_grads(
@@ -354,11 +353,12 @@
     pl.semaphore_wait(across_sem, 3)
     partner = (l + 1 - 2 * core, a)
     pair = []
-    for k in range(1, INSIDE + 1):
-        slot = lax.rem(rank + k, INSIDE)
+    for k in range(1, 5):
+        group = lax.rem(rank // 4 + k, 4)
+        four_rows = pl.ds(pl.multiple_of(group * 4, 4), 4)
         copy = pltpu.make_async_remote_copy(
-            src_ref=w_out.at[1 - core, slot],
-            dst_ref=w_in.at[slot],
+            src_ref=w_out.at[1 - core, four_rows],
+            dst_ref=w_in.at[four_rows],
             send_sem=pair_send,
             recv_sem=pair_recv.at[k - 1],
             device_id=partner,
@@ -367,22 +367,24 @@
         copy.start()
         pair.append(copy)
 
-    for k in range(1, INSIDE + 1):
-        slot = lax.rem(rank + k, INSIDE)
+    for k in range(1, 5):
+        group = lax.rem(rank // 4 + k, 4)
         pair[k - 1].wait_recv()
-        both = (w_out[core, slot].astype(F32) + w_in[slot].astype(F32)).astype(BF)
-        if k == INSIDE:
-            w1[slot] = both
-        else:
-            w_half[slot] = both
-            pltpu.make_async_remote_copy(
-                src_ref=w_half.at[slot],
-                dst_ref=w1.at[rank],
-                send_sem=w1_send,
-                recv_sem=w1_recv,
-                device_id=inside[2](slot),
-                device_id_type=MESH,
-            ).start()
+        for j in range(1, 5):
+            slot = group * 4 + lax.rem(rank + j, 4)
+            both = (w_out[core, slot].astype(F32) + w_in[slot].astype(F32)).astype(BF)
+            if k == 4 and j == 4:
+                w1[rank] = both
+            else:
+                w_half[slot] = both
+                pltpu.make_async_remote_copy(
+                    src_ref=w_half.at[slot],
+                    dst_ref=w1.at[rank],
+                    send_sem=w1_send,
+                    recv_sem=w1_recv,
+                    device_id=inside[2](slot),
+                    device_id_type=MESH,
+                ).start()
 
     tflat[...] = jnp.zeros_like(tflat)
     fold_bias(gs, shear, stacked, xs, tflat)
@@ -410,8 +412,8 @@
         back.append(copy)
     quads_in[0] = quads_out[0]
 
-    for copy in halo:
-        copy.wait_send()
+    wait_bytes(field_in.at[1:], halo_send.at[0])
+    wait_bytes(grad_in.at[1:], halo_send.at[1])
     wait_bytes(w_in, pair_send)
 
     wait_bytes(w1.at[1:], w1_recv)
@@ -494,7 +496,7 @@
         pltpu.VMEM((TOK, 128), BF),
         pltpu.VMEM((4, 3, 6, 2, D), BF),
         pltpu.VMEM((4, 3, 6, 2, D), BF),
-        pltpu.VMEM((4, 72, 128), F32),
+        pltpu.VMEM((4, 96, 128), F32),
         pltpu.VMEM((HEADS, TOK, TOK), F32),
         pltpu.VMEM((HEADS, TOK, TOK), F32),
         pltpu.VMEM((LON, 72, TOK), F32),
@@ -520,12 +522,12 @@
         dma((3,)),
         dma((9,)),
         dma((2,)),
-        dma((8,)),
-        dma((8,)),
+        dma((2,)),
+        dma((2,)),
         dma((4,)),
         dma((4,)),
         dma,
-        dma((INSIDE,)),
+        dma((4,)),
         *([dma] * 5),
         dma((INSIDE,)),
         *([dma] * 8),

time: 45.9 us -> 45.5 us (level)
  no operation moved by 1% of the time
where the time goes in v5:
time: 45.5 us; the launch traced here: 45.4 us
  Pallas kernels  44.7 us (98%)
  between operations  0.64 us (1%)
    pallas_call x1, Pallas kernels, body(): pl.pallas_call(kernel, out_shape=(jax.ShapeDtypeStruct((2, INSIDE, ROWS,...  42.6 us
    pallas_call x1, Pallas kernels, body(): pl.pallas_call(finish, out_shape=(jax.ShapeDtypeStruct((6, 12, 2, D), BF)...  2.2 us

profile of v5, /device:TPU:1, one launch (start us, length us, event | category | flops | bytes accessed | tf_op | source)
XLA Modules:
  0.0 45.4 jit_solution(5417872225872833286)
XLA Ops:
  0.6 42.6 %shard_map.146 = (bf16[2,16,36,128]{3,2,1,0:T(8,128)(2,1)}, bf16[4,3,6,2,192]{4,3,2,1,0:T(2,128)(2,1)}, bf16[16,16,128]{2,1,0:T(8,128)(2,1)}) custom-call(bf16[6,12,2,192]{3,2,1,0:T(2,128)(2,1)} %bitcast.11, bf16[6,12,2,192]{3,2,1,0:T(2,128)(2,1)} %bitcast.8, s32[6,2,12]{2,1,0:T(2,128)} %bitcast.12, f32[192]{0:T(256)} %gain.1, bf16[192,576]{1,0:T(8,128)(2,1)} %wqkv.1, ...), custom_call_target="tpu_custom_call" | custom-call | tf_op jit(solution)/shard_map/pallas_call | solution.py:535
  43.2 2.2 %shard_map.147 = (bf16[6,12,2,192]{3,2,1,0:T(2,128)(2,1)}, f32[192,576]{1,0:T(8,128)}, f32[192,192]{1,0:T(8,128)}, f32[192]{0:T(256)}, f32[6,1,3312]{2,1,0:T(1,128)}) custom-call(bf16[2,16,36,128]{3,2,1,0:T(8,128)(2,1)} %get-tuple-element.13.rows, bf16[4,3,6,2,192]{4,3,2,1,0:T(2,128)(2,1)} %get-tuple-element.14.quads, ...), custom_call_target="tpu_custom_call" | custom-call | tf_op jit(solution)/shard_map/pallas_call | solution.py:552

commit v6 on v5

--- a/solution.py
+++ b/solution.py
@@ -230,20 +230,16 @@
 
 def exchange(src_of, recv, group, send_sem, recv_sem):
     size, rank, device_of = group
-    copies = []
     for k in range(1, size):
         peer = lax.rem(rank + k, size)
-        copy = pltpu.make_async_remote_copy(
+        pltpu.make_async_remote_copy(
             src_ref=src_of(peer),
             dst_ref=recv.at[rank],
             send_sem=send_sem,
-            recv_sem=recv_sem.at[k] if len(recv_sem.shape) else recv_sem,
+            recv_sem=recv_sem,
             device_id=device_of(peer),
             device_id_type=MESH,
-        )
-        copy.start()
-        copies.append(copy)
-    return copies
+        ).start()
 
 
 def wait_bytes(ref, sem):
@@ -287,13 +283,30 @@
     far = ((far_l, a), (l, far_a), (far_l, far_a))
     beside = [(near_l, a), (far_l, a), near[2], far[2]]
     column = [(l, lax.rem(a + k, 8)) for k in range(1, 8)]
-    four = [(block * FOUR + lax.rem(part + k, FOUR), a) for k in range(1, FOUR)]
+    aside = (block * FOUR + lax.rem(part + 2, FOUR), a)
+    partner = (l + 1 - 2 * core, a)
     high, low = block // 4, lax.rem(block, 4)
     lows = [((high * 4 + lax.rem(low + k, 4)) * FOUR + part, a) for k in range(1, 4)]
     highs = [((lax.rem(high + k, 4) * 4 + low) * FOUR + part, a) for k in range(1, 4)]
-    entry = highs + lows + column + beside + four
+    entry = highs + lows + column + beside + [aside]
     for device in entry:
         pl.semaphore_signal(barrier, inc=1, device_id=device, device_id_type=MESH)
+    pl.semaphore_wait(barrier, len(entry))
+
+    for s in range(1, 4):
+        rows = slice(0, 3) if s >= 2 else slice(3, 6)
+        cols = slice(0, 6) if s % 2 else slice(6, 12)
+        for k, (src, dst) in enumerate(((fields, field_in), (grad_out, grad_in))):
+            copy = pltpu.make_async_remote_copy(
+                src_ref=src.at[rows, cols],
+                dst_ref=dst.at[s],
+                send_sem=halo_send.at[k],
+                recv_sem=halo_recv.at[k],
+                device_id=near[s - 1],
+                device_id_type=MESH,
+            )
+            copy.start()
+
     loads = []
     pairs = (
         (table_hbm, table), (shear_hbm, shear), (ids_hbm, ids), (row_hbm, row_of), (lon_hbm, lon_of),
@@ -308,23 +321,7 @@
         own = pltpu.make_async_copy(src.at[3:6, 6:12], dst.at[0], own_sem.at[k])
         own.start()
         owns.append(own)
-    pl.semaphore_wait(barrier, len(entry))
-
-    for s in range(1, 4):
-        rows = slice(0, 3) if s >= 2 else slice(3, 6)
-        cols = slice(0, 6) if s % 2 else slice(6, 12)
-        for k, (src, dst) in enumerate(((fields, field_in), (grad_out, grad_in))):
-            copy = pltpu.make_async_remote_copy(
-                src_ref=src.at[rows, cols],
-                dst_ref=dst.at[s],
-                send_sem=halo_send.at[k],
-                recv_sem=halo_recv.at[k],
-                device_id=near[s - 1],
-                device_id_type=MESH,
-            )
-            copy.start()
-
-    for device in four:
+    for device in (aside, partner):
         pl.semaphore_signal(block_sem, inc=1, device_id=device, device_id_type=MESH)
     for device in highs:
         pl.semaphore_signal(across_sem, inc=1, device_id=device, device_id_type=MESH)
@@ -349,9 +346,8 @@
 
     pack_weights(grad_qkv, grad_proj, flat, w_out)
     rank = inside[1]
-    pl.semaphore_wait(block_sem, FOUR - 1)
+    pl.semaphore_wait(block_sem, 2)
     pl.semaphore_wait(across_sem, 3)
-    partner = (l + 1 - 2 * core, a)
     pair = []
     for k in range(1, 5):
         group = lax.rem(rank // 4 + k, 4)
@@ -439,19 +435,19 @@
 
     wait_bytes(w2.at[1:], w2_recv)
     w3[core, rank] = total_of(w2).astype(BF)
-    c3 = exchange(lambda r: w3.at[core, rank], w3.at[core], inside, w3_send, w3_recv)
+    exchange(lambda r: w3.at[core, rank], w3.at[core], inside, w3_send, w3_recv.at[rank // 4])
     for copy in back:
         copy.wait_send()
     wait_bytes(w2.at[1:], w2_send)
     wait_bytes(t2.at[1:], t2_send)
 
-    for k in range(INSIDE):
-        if k:
-            c3[k - 1].wait_recv()
-        slot = lax.rem(rank + INSIDE - k, INSIDE)
+    for k in range(1, 5):
+        group = lax.rem(rank // 4 + 4 - k, 4)
+        wait_bytes(w1.at[0:4] if k < 4 else w1.at[0:3], w3_recv.at[group])
+        four_rows = pl.ds(pl.multiple_of(group * 4, 4), 4)
         pltpu.make_async_remote_copy(
-            src_ref=w3.at[core, slot],
-            dst_ref=out_flat.at[core, slot],
+            src_ref=w3.at[core, four_rows],
+            dst_ref=out_flat.at[core, four_rows],
             send_sem=w4_send,
             recv_sem=w4_recv,
             device_id=partner,
@@ -529,7 +525,7 @@
         dma,
         dma((4,)),
         *([dma] * 5),
-        dma((INSIDE,)),
+        dma((4,)),
         *([dma] * 8),
     ]
     rows, quads, trows = pl.pallas_call(

time: 45.5 us -> 45.5 us (level)
  no operation moved by 1% of the time
where the time goes in v6:
time: 45.5 us; the launch traced here: 45.3 us
  Pallas kernels  44.7 us (98%)
  between operations  0.64 us (1%)
    pallas_call x1, Pallas kernels, body(): pl.pallas_call(kernel, out_shape=(jax.ShapeDtypeStruct((2, INSIDE, ROWS,...  42.5 us
    pallas_call x1, Pallas kernels, body(): pl.pallas_call(finish, out_shape=(jax.ShapeDtypeStruct((6, 12, 2, D), BF)...  2.2 us

profile of v6, /device:TPU:1, one launch (start us, length us, event | category | flops | bytes accessed | tf_op | source)
XLA Modules:
  0.0 45.3 jit_solution(13767305765578148612)
XLA Ops:
  0.6 42.5 %shard_map.146 = (bf16[2,16,36,128]{3,2,1,0:T(8,128)(2,1)}, bf16[4,3,6,2,192]{4,3,2,1,0:T(2,128)(2,1)}, bf16[16,16,128]{2,1,0:T(8,128)(2,1)}) custom-call(bf16[6,12,2,192]{3,2,1,0:T(2,128)(2,1)} %bitcast.11, bf16[6,12,2,192]{3,2,1,0:T(2,128)(2,1)} %bitcast.8, s32[6,2,12]{2,1,0:T(2,128)} %bitcast.12, f32[192]{0:T(256)} %gain.1, bf16[192,576]{1,0:T(8,128)(2,1)} %wqkv.1, ...), custom_call_target="tpu_custom_call" | custom-call | tf_op jit(solution)/shard_map/pallas_call | solution.py:531
  43.1 2.2 %shard_map.147 = (bf16[6,12,2,192]{3,2,1,0:T(2,128)(2,1)}, f32[192,576]{1,0:T(8,128)}, f32[192,192]{1,0:T(8,128)}, f32[192]{0:T(256)}, f32[6,1,3312]{2,1,0:T(1,128)}) custom-call(bf16[2,16,36,128]{3,2,1,0:T(8,128)(2,1)} %get-tuple-element.13.rows, bf16[4,3,6,2,192]{4,3,2,1,0:T(2,128)(2,1)} %get-tuple-element.14.quads, ...), custom_call_target="tpu_custom_call" | custom-call | tf_op jit(solution)/shard_map/pallas_call | solution.py:548
